TPU v7x, 32 devices: a whole 2x2x4 slice. The times are simulated.
32 devices in a mesh: pipe: 4 (over x, core), dp: 2 (over y), tensor: 4 (over z).
Axes of the slice: x: 2, y: 2, z: 4, core: 2. Of those that a mesh axis runs over, the one named last changes fastest.
Arguments:
- section_inputs: bfloat16 [4, 1024, 4096], P('pipe', ('dp', 'tensor')), may hold values from -36 to 36
- norm_gain: bfloat16 [4, 4096], P('pipe'), may hold values from 0.5 to 1.5
- query_weight: bfloat16 [4, 4096, 4096], P('pipe', None, 'tensor'), may hold values from -0.09375 to 0.09375
- key_weight: bfloat16 [4, 4096, 512], P('pipe', None, 'tensor'), may hold values from -0.09375 to 0.09375
- value_weight: bfloat16 [4, 4096, 512], P('pipe', None, 'tensor'), may hold values from -0.09375 to 0.09375
- output_weight: bfloat16 [4, 4096, 4096], P('pipe', 'tensor'), may hold values from -0.09375 to 0.09375
- upstream_grad: bfloat16 [1024, 4096], P(('dp', 'tensor')), may hold values from -6 to 6
- document_ids: int32 [2, 512], P('dp'), may hold values from 0 to 3, never falling along the last dimension, each value on 1 to 256 neighbouring positions
Outputs:
- input_grads: bfloat16 [4, 1024, 4096], P('pipe', ('dp', 'tensor'))
- query_grads: float32 [4, 4096, 4096], P('pipe', 'dp', 'tensor')
- key_grads: float32 [4, 4096, 512], P('pipe', 'dp', 'tensor')
- value_grads: float32 [4, 4096, 512], P('pipe', 'dp', 'tensor')
- output_grads: float32 [4, 4096, 4096], P('pipe', 'tensor', 'dp')
Inputs may be any that keep to these rules, and one draw needn't show every extreme that they name: `document_ids`: along each sequence the document numbers never fall; each of the 4 documents holds 1 to 256 tokens, one of them exactly 256.
All inputs are finite; a program needn't handle non-finite values.
Results may differ from a plain program's by a relative error of at most 0.03.
Values may be sent and summed in bfloat16 or wider, within the bound.
A program may use at most 256 MiB of HBM per device.

v0:
```python
import math

import jax
import jax.numpy as jnp
from jax import lax
from jax.sharding import PartitionSpec as P

HD = 128


epsilon = 1e-05
rope_base = 500000.0


def shifted(shard, axis, by):
    devices = lax.axis_size(axis)
    pairs = [(i, i + by) for i in range(devices) if 0 <= i + by < devices]
    return lax.ppermute(shard, axis, pairs)


def position_tables(document_ids, head_dim):
    seq_len = document_ids.shape[1]
    index = jnp.arange(seq_len, dtype=jnp.int32)
    earlier = (document_ids[:, None, :] < document_ids[:, :, None]).astype(jnp.int32)
    position = index[None, :] - jnp.sum(earlier, axis=2)
    half = head_dim // 2
    expo = jnp.arange(half, dtype=jnp.float32) * (2.0 / head_dim)
    freq = jnp.exp(expo * -math.log(rope_base))
    angle = position.astype(jnp.float32)[:, :, None] * freq
    same = document_ids[:, :, None] == document_ids[:, None, :]
    causal = index[:, None] >= index[None, :]
    visible = jnp.logical_and(same, causal[None])
    return (jnp.cos(angle), jnp.sin(angle), visible)


def rotate(vector, rot_cos, rot_sin, direction):
    half = vector.shape[-1] // 2
    first = vector[..., :half]
    second = vector[..., half:]
    return jnp.concatenate(
        [
            first * rot_cos - direction * second * rot_sin,
            second * rot_cos + direction * first * rot_sin,
        ],
        axis=-1,
    )


def normalize(rows, gain):
    values = rows.astype(jnp.float32)
    inverse = lax.rsqrt(jnp.mean(values * values, axis=-1, keepdims=True) + epsilon)
    unit_rows = values * inverse
    normed = (unit_rows * gain.astype(jnp.float32)).astype(jnp.bfloat16)
    return (inverse, unit_rows, normed)


def attention_forward(query_rot, key_rot, value_low, visible):
    scale = 1.0 / math.sqrt(HD)
    scores = (
        jnp.einsum("bqngd,bknd->bngqk", query_rot, key_rot, preferred_element_type=jnp.float32)
        * scale
    )
    expo = jnp.where(visible[:, None, None], jnp.exp(scores), 0.0)
    prob = expo / jnp.sum(expo, axis=-1, keepdims=True)
    prob_low = prob.astype(jnp.bfloat16)
    mixed = jnp.einsum("bngqk,bknd->bqngd", prob_low, value_low, preferred_element_type=jnp.float32)
    return (prob, prob_low, mixed.astype(jnp.bfloat16))


def attention_backward(grad_mixed, query_rot, key_rot, value_low, prob, prob_low, rot_cos, rot_sin):
    scale = 1.0 / math.sqrt(HD)
    grad_value = jnp.einsum(
        "bngqk,bqngd->bknd", prob_low, grad_mixed, preferred_element_type=jnp.float32
    )
    grad_prob = jnp.einsum(
        "bqngd,bknd->bngqk", grad_mixed, value_low, preferred_element_type=jnp.float32
    )
    grad_score = prob * (grad_prob - jnp.sum(grad_prob * prob, axis=-1, keepdims=True)) * scale
    score_low = grad_score.astype(jnp.bfloat16)
    grad_query = jnp.einsum(
        "bngqk,bknd->bqngd", score_low, key_rot, preferred_element_type=jnp.float32
    )
    grad_key = jnp.einsum(
        "bngqk,bqngd->bknd", score_low, query_rot, preferred_element_type=jnp.float32
    )
    grad_query = rotate(
        grad_query, rot_cos[:, :, None, None, :], rot_sin[:, :, None, None, :], -1.0
    )
    grad_key = rotate(grad_key, rot_cos[:, :, None, :], rot_sin[:, :, None, :], -1.0)
    return (
        grad_query.astype(jnp.bfloat16),
        grad_key.astype(jnp.bfloat16),
        grad_value.astype(jnp.bfloat16),
    )


def back_norm(grad_normed, unit_rows, inverse, gain, incoming):
    grad_unit = grad_normed * gain.astype(jnp.float32)
    branch = (
        grad_unit - unit_rows * jnp.mean(grad_unit * unit_rows, axis=-1, keepdims=True)
    ) * inverse
    return (incoming.astype(jnp.float32) + branch).astype(jnp.bfloat16)


def local(
    section_inputs,
    norm_gain,
    query_weight,
    key_weight,
    value_weight,
    output_weight,
    upstream_grad,
    document_ids,
):
    pipes = lax.axis_size("pipe")
    section = lax.axis_index("pipe")
    groups = lax.axis_size("dp")
    width = section_inputs.shape[2]
    seq_len = document_ids.shape[1]
    q_width = query_weight.shape[2]
    k_width = key_weight.shape[2]
    kv_local = k_width // HD
    group = q_width // k_width
    gain = norm_gain[0]
    w_query = query_weight[0]
    w_key = key_weight[0]
    w_value = value_weight[0]
    w_output = output_weight[0]
    rot_cos, rot_sin, visible = position_tables(document_ids, HD)
    last = pipes - 1
    inverse, unit_rows, normed_shard = normalize(section_inputs[0], gain)
    normed = lax.all_gather(normed_shard, "tensor", axis=0, tiled=True)
    incoming = jnp.where(section == last, upstream_grad, jnp.zeros_like(upstream_grad))
    query = jnp.dot(normed, w_query, preferred_element_type=jnp.float32).reshape(
        1, seq_len, kv_local, group, HD
    )
    keys = jnp.dot(normed, w_key, preferred_element_type=jnp.float32).reshape(
        1, seq_len, kv_local, HD
    )
    values = jnp.dot(normed, w_value, preferred_element_type=jnp.float32).reshape(
        1, seq_len, kv_local, HD
    )
    query_rot = rotate(
        query, rot_cos[:, :, None, None, :], rot_sin[:, :, None, None, :], 1.0
    ).astype(jnp.bfloat16)
    key_rot = rotate(keys, rot_cos[:, :, None, :], rot_sin[:, :, None, :], 1.0).astype(jnp.bfloat16)
    value_low = values.astype(jnp.bfloat16)
    prob, prob_low, mixed = attention_forward(query_rot, key_rot, value_low, visible)
    mixed_flat = mixed.reshape(seq_len, q_width)

    def backward_turn(cotangent):
        grad_mixed = jnp.einsum(
            "sd,hd->sh", cotangent, w_output, preferred_element_type=jnp.float32
        )
        grad_mixed = grad_mixed.astype(jnp.bfloat16).reshape(1, seq_len, kv_local, group, HD)
        grad_query, grad_key, grad_value = attention_backward(
            grad_mixed, query_rot, key_rot, value_low, prob, prob_low, rot_cos, rot_sin
        )
        flat_query = grad_query.reshape(seq_len, q_width)
        flat_key = grad_key.reshape(seq_len, k_width)
        flat_value = grad_value.reshape(seq_len, k_width)
        grad_normed = (
            jnp.einsum("sh,dh->sd", flat_query, w_query, preferred_element_type=jnp.float32)
            + jnp.einsum("sh,dh->sd", flat_key, w_key, preferred_element_type=jnp.float32)
            + jnp.einsum("sh,dh->sd", flat_value, w_value, preferred_element_type=jnp.float32)
        )
        return (grad_normed.astype(jnp.bfloat16), flat_query, flat_key, flat_value)

    def skipped_turn(cotangent):
        return (
            jnp.zeros((seq_len, width), jnp.bfloat16),
            jnp.zeros((seq_len, q_width), jnp.bfloat16),
            jnp.zeros((seq_len, k_width), jnp.bfloat16),
            jnp.zeros((seq_len, k_width), jnp.bfloat16),
        )

    saved_query = jnp.zeros((seq_len, q_width), jnp.bfloat16)
    saved_key = jnp.zeros((seq_len, k_width), jnp.bfloat16)
    saved_value = jnp.zeros((seq_len, k_width), jnp.bfloat16)
    saved_cot = jnp.zeros((seq_len, width), jnp.bfloat16)
    saved_input = jnp.zeros_like(incoming)
    for turn in range(pipes):
        active = section == last - turn
        cotangent = lax.all_gather(incoming, "tensor", axis=0, tiled=True)
        grad_normed, flat_query, flat_key, flat_value = lax.cond(
            active, backward_turn, skipped_turn, cotangent
        )
        summed = lax.psum_scatter(grad_normed, "tensor", scatter_dimension=0, tiled=True).astype(
            jnp.float32
        )
        result = back_norm(summed, unit_rows, inverse, gain, incoming)
        saved_query = jnp.where(active, flat_query, saved_query)
        saved_key = jnp.where(active, flat_key, saved_key)
        saved_value = jnp.where(active, flat_value, saved_value)
        saved_cot = jnp.where(active, cotangent, saved_cot)
        saved_input = jnp.where(active, result, saved_input)
        if turn + 1 < pipes:
            incoming = shifted(result, "pipe", -1)
    scale_out = 1.0 / math.sqrt(groups * seq_len)
    terms = (
        jnp.einsum("sd,sh->dh", normed, saved_query, preferred_element_type=jnp.float32).astype(
            jnp.bfloat16
        ),
        jnp.einsum("sd,sh->dh", normed, saved_key, preferred_element_type=jnp.float32).astype(
            jnp.bfloat16
        ),
        jnp.einsum("sd,sh->dh", normed, saved_value, preferred_element_type=jnp.float32).astype(
            jnp.bfloat16
        ),
        jnp.einsum("sh,sd->hd", mixed_flat, saved_cot, preferred_element_type=jnp.float32).astype(
            jnp.bfloat16
        ),
    )
    sums = (
        lax.psum_scatter(terms[0], "dp", scatter_dimension=0, tiled=True).astype(jnp.float32),
        lax.psum_scatter(terms[1], "dp", scatter_dimension=0, tiled=True).astype(jnp.float32),
        lax.psum_scatter(terms[2], "dp", scatter_dimension=0, tiled=True).astype(jnp.float32),
        lax.psum_scatter(terms[3], "dp", scatter_dimension=1, tiled=True).astype(jnp.float32),
    )
    query_grads = (sums[0] * scale_out)[None]
    key_grads = (sums[1] * scale_out)[None]
    value_grads = (sums[2] * scale_out)[None]
    output_grads = (sums[3] * scale_out)[None]
    return (saved_input[None], query_grads, key_grads, value_grads, output_grads)


def solution(mesh):
    placed = (
        P("pipe", ("dp", "tensor"), None),
        P("pipe", None),
        P("pipe", None, "tensor"),
        P("pipe", None, "tensor"),
        P("pipe", None, "tensor"),
        P("pipe", "tensor", None),
        P(("dp", "tensor"), None),
        P("dp", None),
    )
    return jax.shard_map(
        local,
        mesh=mesh,
        in_specs=placed,
        out_specs=(
            P("pipe", ("dp", "tensor"), None),
            P("pipe", "dp", "tensor"),
            P("pipe", "dp", "tensor"),
            P("pipe", "dp", "tensor"),
            P("pipe", "tensor", "dp"),
        ),
        check_vma=False,
    )
```

profile of v0, /device:TPU:8, one launch (start us, length us, event | category | flops | bytes accessed | tf_op | source)
XLA Modules:
  0.0 1252.1 jit_solution(392810936247310694)
XLA Ops:
  13.3 12.1 copy.92
  27.0 64.6 %all-gather.8.cloned.1.call-done = bf16[512,4096]{1,0:T(8,128)(2,1)} async-done(((bf16[128,4096]{1,0:T(8,128)(2,1)}), bf16[512,4096]{1,0:T(8,128)(2,1)}) %all-gather.8.cloned.1.call-update) | async-done | bytes 4194320 | tf_op jit(solution)/shard_map/all_gather | solution.py:132
  96.6 7.3 fusion.122
  114.6 58.4 %all-gather.6.cloned.1.call-done = bf16[512,4096]{1,0:T(8,128)(2,1)} async-done(((bf16[128,4096]{1,0:T(8,128)(2,1)}), bf16[512,4096]{1,0:T(8,128)(2,1)}) %all-gather.6.cloned.1.call-update) | async-done | bytes 4194320 | tf_op jit(solution)/shard_map/all_gather | solution.py:184
  173.0 14.0 %conditional.4 = (bf16[512,4096]{1,0:T(8,128)(2,1)}, bf16[512,1024]{0,1:T(8,128)(2,1)}, bf16[512,128]{0,1:T(8,128)(2,1)}, bf16[512,128]{0,1:T(8,128)(2,1)}) conditional(s32[]{:T(128)} %convert_element_type.262, () %tuple.40, (bf16[512,4096]{1,0:T(8,128)(2,1)}, bf16[1024,4096]{1,0:T(8,128)(2,1)}, bf16[1,512,1,128]{3,1,2,0:T(8,128)(2,1)S(1)}, ...), branch_computations={%region_3.4_spmd, %region_4.6_spmd} | conditional | flops 11835437056 | bytes 208961792 | solution.py:185
  187.1 114.4 %reduce-scatter.9.cloned.1.call-done = bf16[128,4096]{1,0:T(8,128)(2,1)} async-done(((bf16[512,4096]{1,0:T(8,128)(2,1)}), bf16[128,4096]{1,0:T(8,128)(2,1)}) %reduce-scatter.9.cloned.1.call-update) | async-done | bytes 1048592 | tf_op jit(solution)/shard_map/reduce_scatter | solution.py:188
  311.0 88.9 %all-gather.10.cloned.1.call-done = bf16[512,4096]{1,0:T(8,128)(2,1)} async-done(((bf16[128,4096]{1,0:T(8,128)(2,1)}), bf16[512,4096]{1,0:T(8,128)(2,1)}) %all-gather.10.cloned.1.call-update) | async-done | bytes 4194320 | tf_op jit(solution)/shard_map/all_gather | solution.py:184
  399.9 13.8 %conditional.5 = (bf16[512,4096]{1,0:T(8,128)(2,1)}, bf16[512,1024]{0,1:T(8,128)(2,1)}, bf16[512,128]{0,1:T(8,128)(2,1)}, bf16[512,128]{0,1:T(8,128)(2,1)}) conditional(s32[]{:T(128)} %convert_element_type.274, () %tuple.42, (bf16[512,4096]{1,0:T(8,128)(2,1)}, bf16[1024,4096]{1,0:T(8,128)(2,1)}, bf16[1,512,1,128]{3,1,2,0:T(8,128)(2,1)S(1)}, ...), branch_computations={%region_8.9_spmd, %region_9.11_spmd} | conditional | flops 11835437056 | bytes 187990240 | solution.py:185
  413.8 116.1 %reduce-scatter.11.cloned.1.call-done = bf16[128,4096]{1,0:T(8,128)(2,1)} async-done(((bf16[512,4096]{1,0:T(8,128)(2,1)}), bf16[128,4096]{1,0:T(8,128)(2,1)}) %reduce-scatter.11.cloned.1.call-update) | async-done | bytes 1048592 | tf_op jit(solution)/shard_map/reduce_scatter | solution.py:188
  539.7 88.9 %all-gather.12.cloned.1.call-done = bf16[512,4096]{1,0:T(8,128)(2,1)} async-done(((bf16[128,4096]{1,0:T(8,128)(2,1)}), bf16[512,4096]{1,0:T(8,128)(2,1)}) %all-gather.12.cloned.1.call-update) | async-done | bytes 4194320 | tf_op jit(solution)/shard_map/all_gather | solution.py:184
  628.6 15.2 %conditional.6 = (bf16[512,4096]{1,0:T(8,128)(2,1)}, bf16[512,1024]{0,1:T(8,128)(2,1)}, bf16[512,128]{0,1:T(8,128)(2,1)}, bf16[512,128]{0,1:T(8,128)(2,1)}) conditional(s32[]{:T(128)} %convert_element_type.278, () %tuple.44, (bf16[512,4096]{1,0:T(8,128)(2,1)}, bf16[1024,4096]{1,0:T(8,128)(2,1)}, bf16[1,512,1,128]{3,1,2,0:T(8,128)(2,1)S(1)}, ...), branch_computations={%region_13.14_spmd, %region_14.16_spmd} | conditional | flops 11835437056 | bytes 187990240 | solution.py:185
  643.9 113.4 %reduce-scatter.13.cloned.1.call-done = bf16[128,4096]{1,0:T(8,128)(2,1)} async-done(((bf16[512,4096]{1,0:T(8,128)(2,1)}), bf16[128,4096]{1,0:T(8,128)(2,1)}) %reduce-scatter.13.cloned.1.call-update) | async-done | bytes 1048592 | tf_op jit(solution)/shard_map/reduce_scatter | solution.py:188
  767.1 88.9 %all-gather.14.cloned.1.call-done = bf16[512,4096]{1,0:T(8,128)(2,1)} async-done(((bf16[128,4096]{1,0:T(8,128)(2,1)}), bf16[512,4096]{1,0:T(8,128)(2,1)}) %all-gather.14.cloned.1.call-update) | async-done | bytes 4194320 | tf_op jit(solution)/shard_map/all_gather | solution.py:184
  856.1 50.5 %conditional.7 = (bf16[512,4096]{1,0:T(8,128)(2,1)}, bf16[512,1024]{0,1:T(8,128)(2,1)}, bf16[512,128]{0,1:T(8,128)(2,1)}, bf16[512,128]{0,1:T(8,128)(2,1)}) conditional(s32[]{:T(128)} %convert_element_type.282, () %tuple.46, (bf16[512,4096]{1,0:T(8,128)(2,1)}, bf16[1024,4096]{1,0:T(8,128)(2,1)}, bf16[1,512,1,128]{3,1,2,0:T(8,128)(2,1)S(1)}, ...), branch_computations={%region_18.19_spmd, %region_19.21_spmd} | conditional | flops 11835437056 | bytes 213156128 | solution.py:185
  856.1 8.0 copy.78
  864.7 9.7 convolution_convert_fusion.3
  880.9 8.1 fusion.61
  916.6 10.9 convolution_convert_fusion.5
  931.3 9.5 convolution_convert_fusion.4
  943.1 11.2 reduce-scatter.21.cloned.1.call-done
  956.4 77.7 %reduce-scatter.15.cloned.1.call-done = bf16[128,4096]{1,0:T(8,128)(2,1)} async-done(((bf16[512,4096]{1,0:T(8,128)(2,1)}), bf16[128,4096]{1,0:T(8,128)(2,1)}) %reduce-scatter.15.cloned.1.call-update) | async-done | bytes 1048592 | tf_op jit(solution)/shard_map/reduce_scatter | solution.py:188
  1039.6 97.0 %reduce-scatter.17.cloned.1.call-done = bf16[2048,1024]{1,0:T(8,128)(2,1)} async-done(((bf16[4096,1024]{1,0:T(8,128)(2,1)}), bf16[2048,1024]{1,0:T(8,128)(2,1)}) %reduce-scatter.17.cloned.1.call-update) | async-done | bytes 4194320 | tf_op jit(solution)/shard_map/reduce_scatter | solution.py:215
  1136.6 6.8 multiply_bitcast_fusion.5
  1143.4 94.9 %reduce-scatter.23.cloned.1.call-done = bf16[1024,2048]{1,0:T(8,128)(2,1)} async-done(((bf16[1024,4096]{1,0:T(8,128)(2,1)}), bf16[1024,2048]{1,0:T(8,128)(2,1)}) %reduce-scatter.23.cloned.1.call-update) | async-done | bytes 4194320 | tf_op jit(solution)/shard_map/reduce_scatter | solution.py:218
  (143 shorter events, 121.9 us)
Async XLA Ops:
  7.2 84.4 %all-gather.8.cloned.1.call-start = ((), (), s32[]{:S(2)}) async-start(), calls=%async_computation.9 | async-start | bytes 5242880 | tf_op jit(solution)/shard_map/all_gather | solution.py:132
  8.8 750.3 %copy-start.29 = (f32[128]{0:T(128)}, f32[128]{0:T(128)S(1)}, u32[]{:S(2)}) copy-start(f32[128]{0:T(128)S(1)} %add_rsqrt_fusion) | copy-start | bytes 1540
  12.1 160.9 %all-gather.6.cloned.1.call-start = ((), (), s32[]{:S(2)}) async-start(), calls=%async_computation.8 | async-start | bytes 5242880 | tf_op jit(solution)/shard_map/all_gather | solution.py:184
  13.3 288.2 %reduce-scatter.9.cloned.1.call-start = ((), (), s32[]{:S(2)}) async-start(), calls=%async_computation.10 | async-start | bytes 5242880 | tf_op jit(solution)/shard_map/reduce_scatter | solution.py:188
  13.3 12.1 copy-start.31
  13.3 78.2 %copy-start.2 = (bf16[1,4096,128]{2,1,0:T(8,128)(2,1)S(1)}, bf16[1,4096,128]{2,1,0:T(8,128)(2,1)}, u32[]{:S(2)}) copy-start(bf16[1,4096,128]{2,1,0:T(8,128)(2,1)} %param.19) | copy-start | bytes 3145732
  187.0 114.5 %copy-start = (bf16[1,128,4096]{2,1,0:T(8,128)(2,1)S(1)}, bf16[1,128,4096]{2,1,0:T(8,128)(2,1)}, u32[]{:S(2)}) copy-start(bf16[1,128,4096]{2,1,0:T(8,128)(2,1)} %param.16) | copy-start | bytes 3145732
  187.0 212.8 %all-gather.10.cloned.1.call-start = ((), (), s32[]{:S(2)}) async-start(), calls=%async_computation.11 | async-start | bytes 5242880 | tf_op jit(solution)/shard_map/all_gather | solution.py:184
  306.2 4.7 collective-permute-start
  310.9 219.0 %reduce-scatter.11.cloned.1.call-start = ((), (), s32[]{:S(2)}) async-start(), calls=%async_computation.12 | async-start | bytes 5242880 | tf_op jit(solution)/shard_map/reduce_scatter | solution.py:188
  413.7 214.9 %all-gather.12.cloned.1.call-start = ((), (), s32[]{:S(2)}) async-start(), calls=%async_computation.13 | async-start | bytes 5242880 | tf_op jit(solution)/shard_map/all_gather | solution.py:184
  535.0 4.7 collective-permute-start.1
  539.7 217.7 %reduce-scatter.13.cloned.1.call-start = ((), (), s32[]{:S(2)}) async-start(), calls=%async_computation.14 | async-start | bytes 5242880 | tf_op jit(solution)/shard_map/reduce_scatter | solution.py:188
  643.8 212.2 %all-gather.14.cloned.1.call-start = ((), (), s32[]{:S(2)}) async-start(), calls=%async_computation.15 | async-start | bytes 5242880 | tf_op jit(solution)/shard_map/all_gather | solution.py:184
  762.4 4.7 collective-permute-start.2
  767.1 173.8 %reduce-scatter.19.cloned.1.call-start = ((), (), s32[]{:S(2)}) async-start(), calls=%async_computation.18 | async-start | bytes 1572864 | tf_op jit(solution)/shard_map/reduce_scatter | solution.py:216
  864.0 12.2 slice-start.6
  911.2 43.2 %reduce-scatter.21.cloned.1.call-start = ((), (), s32[]{:S(2)}) async-start(), calls=%async_computation.19 | async-start | bytes 1572864 | tf_op jit(solution)/shard_map/reduce_scatter | solution.py:217
  915.8 118.3 %reduce-scatter.15.cloned.1.call-start = ((), (), s32[]{:S(2)}) async-start(), calls=%async_computation.16 | async-start | bytes 5242880 | tf_op jit(solution)/shard_map/reduce_scatter | solution.py:188
  916.5 220.1 %reduce-scatter.17.cloned.1.call-start = ((), (), s32[]{:S(2)}) async-start(), calls=%async_computation.17 | async-start | bytes 12582912 | tf_op jit(solution)/shard_map/reduce_scatter | solution.py:215
  927.5 310.8 %reduce-scatter.23.cloned.1.call-start = ((), (), s32[]{:S(2)}) async-start(), calls=%async_computation.20 | async-start | bytes 12582912 | tf_op jit(solution)/shard_map/reduce_scatter | solution.py:218
  940.8 93.3 %copy-start.30 = (f32[128]{0:T(128)S(1)}, f32[128]{0:T(128)}, u32[]{:S(2)}) copy-start(f32[128]{0:T(128)} %copy-done.29) | copy-start | bytes 1540
  940.9 95.0 %copy-start.17 = (bf16[128,4096]{1,0:T(8,128)(2,1)S(1)}, bf16[128,4096]{1,0:T(8,128)(2,1)}, u32[]{:S(2)}) copy-start(bf16[128,4096]{1,0:T(8,128)(2,1)} %copy-done.16) | copy-start | bytes 3145732
  940.9 95.0 %copy-start.19 = (bf16[128,4096]{1,0:T(8,128)(2,1)S(1)}, bf16[128,4096]{1,0:T(8,128)(2,1)}, u32[]{:S(2)}) copy-start(bf16[128,4096]{1,0:T(8,128)(2,1)} %copy-done.18) | copy-start | bytes 3145732
  (15 other events, 57.8 us)
Sparse Core Ops, SparseCore 0:
  12.2 79.2 all-gather.7
  93.7 79.2 all-gather.5
  187.2 114.2 reduce-scatter.8
  311.0 88.7 all-gather.9
  413.9 115.9 reduce-scatter.10
  539.8 88.7 all-gather.11
  644.0 113.3 reduce-scatter.12
  767.2 88.8 all-gather.13
  911.3 20.5 reduce-scatter.18
  934.0 20.3 reduce-scatter.20
  957.3 76.7 reduce-scatter.14
  1036.8 99.7 reduce-scatter.16
  1139.0 99.2 reduce-scatter.22
where the time goes:
time: 1260 us; the launch traced here: 1250 us
  waiting for transfers between devices  1030 us (82%)
  matrix products  78.4 us (6%)
  other arithmetic  60.9 us (5%)
  local copies, waits for them, and re-layouts  39.4 us (3%)
  loops' own time  28.7 us (2%)
  between operations  14.7 us (1%)
    reduce_scatter x4, waiting for transfers between devices, local(): lax.psum_scatter(grad_normed, 'tensor', scatter_dimension=0, tiled=True)  422 us
    all_gather x4, waiting for transfers between devices, local(): cotangent = lax.all_gather(incoming, 'tensor', axis=0, tiled=True)  325 us
    reduce_scatter x1, waiting for transfers between devices, local(): lax.psum_scatter(terms[0], 'dp', scatter_dimension=0, tiled=True)  97 us
    reduce_scatter x1, waiting for transfers between devices, local(): lax.psum_scatter(terms[3], 'dp', scatter_dimension=1, tiled=True)  94.9 us
    all_gather x1, waiting for transfers between devices, local(): normed = lax.all_gather(normed_shard, 'tensor', axis=0, tiled=True)  64.6 us
    another operation x14, local copies, waits for them, and re-layouts  34.7 us
    another operation x4, loops' own time, local(): lax.cond(active, backward_turn, skipped_turn, cotangent)  28.7 us
  transfers between devices with their start and end apart: 16, of which 15 were waited for; matrix products, arithmetic and copies ran while one was open for 7% of the time, Pallas kernels for 0%

commit v1 on v0

v1 whole, which is shorter than its diff:
```python
import functools
import math

import jax
import jax.numpy as jnp
from jax import lax
from jax.experimental import pallas as pl
from jax.experimental.pallas import tpu as pltpu
from jax.sharding import PartitionSpec as P

HD = 128

epsilon = 1e-05
rope_base = 500000.0


def position_tables(document_ids, head_dim):
    ids = document_ids[0]
    index = jnp.arange(ids.shape[0], dtype=jnp.int32)
    earlier = (ids[None, :] < ids[:, None]).astype(jnp.int32)
    position = index - jnp.sum(earlier, axis=1)
    half = head_dim // 2
    expo = jnp.arange(half, dtype=jnp.float32) * (2.0 / head_dim)
    freq = jnp.exp(expo * -math.log(rope_base))
    angle = position.astype(jnp.float32)[:, None] * freq
    cos, sin = jnp.cos(angle), jnp.sin(angle)
    same = ids[:, None] == ids[None, :]
    visible = jnp.logical_and(same, index[:, None] >= index[None, :])
    return (
        jnp.concatenate([cos, cos], axis=1),
        jnp.concatenate([-sin, sin], axis=1),
        visible.astype(jnp.float32),
    )


def normalize(rows, gain):
    values = rows.astype(jnp.float32)
    inverse = lax.rsqrt(jnp.mean(values * values, axis=-1, keepdims=True) + epsilon)
    unit_rows = values * inverse
    normed = (unit_rows * gain.astype(jnp.float32)).astype(jnp.bfloat16)
    return (inverse, unit_rows, normed)


def back_norm(grad_normed, unit_rows, inverse, gain, incoming):
    grad_unit = grad_normed * gain.astype(jnp.float32)
    branch = (
        grad_unit - unit_rows * jnp.mean(grad_unit * unit_rows, axis=-1, keepdims=True)
    ) * inverse
    return (incoming.astype(jnp.float32) + branch).astype(jnp.bfloat16)


def dot_nt(left, right):
    return lax.dot_general(
        left, right, (((1,), (1,)), ((), ())), preferred_element_type=jnp.float32
    )


def dot_tn(left, right):
    return lax.dot_general(
        left, right, (((0,), (0,)), ((), ())), preferred_element_type=jnp.float32
    )


def forward_kernel(group, q_ref, k_ref, v_ref, cos_ref, sin_ref, vis_ref,
                   qr_ref, kr_ref, vl_ref, prob_ref, mixed_ref):
    def turned(vector):
        return vector * cos_ref[...] + pltpu.roll(vector, HD // 2, 1) * sin_ref[...]

    @pl.when(lax.rem(pl.program_id(0), group) == 0)
    def _():
        kr_ref[...] = turned(k_ref[...]).astype(jnp.bfloat16)
        vl_ref[...] = v_ref[...].astype(jnp.bfloat16)

    query = turned(q_ref[...]).astype(jnp.bfloat16)
    qr_ref[...] = query
    scores = dot_nt(query, kr_ref[...]) * (1.0 / math.sqrt(HD))
    expo = jnp.where(vis_ref[...] > 0.0, jnp.exp(scores), 0.0)
    prob = (expo / jnp.sum(expo, axis=-1, keepdims=True)).astype(jnp.bfloat16)
    prob_ref[0] = prob
    mixed_ref[...] = jnp.dot(prob, vl_ref[...], preferred_element_type=jnp.float32).astype(
        jnp.bfloat16
    )


def attention_forward(query, keys, values, cos, sin, visible):
    seq, q_width = query.shape
    k_width = keys.shape[1]
    heads, group = q_width // HD, q_width // k_width
    per_head = pl.BlockSpec((seq, HD), lambda h: (0, h))
    per_kv = pl.BlockSpec((seq, HD), lambda h: (0, h // group))
    table = pl.BlockSpec((seq, HD), lambda h: (0, 0))
    square = pl.BlockSpec((seq, seq), lambda h: (0, 0))
    return pl.pallas_call(
        functools.partial(forward_kernel, group),
        grid=(heads,),
        in_specs=[per_head, per_kv, per_kv, table, table, square],
        out_specs=[
            per_head,
            per_kv,
            per_kv,
            pl.BlockSpec((1, seq, seq), lambda h: (h, 0, 0)),
            per_head,
        ],
        out_shape=[
            jax.ShapeDtypeStruct((seq, q_width), jnp.bfloat16),
            jax.ShapeDtypeStruct((seq, k_width), jnp.bfloat16),
            jax.ShapeDtypeStruct((seq, k_width), jnp.bfloat16),
            jax.ShapeDtypeStruct((heads, seq, seq), jnp.bfloat16),
            jax.ShapeDtypeStruct((seq, q_width), jnp.bfloat16),
        ],
        compiler_params=pltpu.CompilerParams(vmem_limit_bytes=32 * 1024 * 1024),
        cost_estimate=pl.CostEstimate(
            flops=4 * heads * seq * seq * HD,
            bytes_accessed=2 * heads * seq * seq + 8 * seq * q_width,
            transcendentals=heads * seq * seq,
        ),
    )(query, keys, values, cos, sin, visible)


def backward_kernel(group, gm_ref, q_ref, k_ref, v_ref, prob_ref, cos_ref, sin_ref,
                    gq_ref, gk_ref, gv_ref, key_total, value_total):
    member = lax.rem(pl.program_id(0), group)

    def turned_back(vector):
        return vector * cos_ref[...] - pltpu.roll(vector, HD // 2, 1) * sin_ref[...]

    @pl.when(member == 0)
    def _():
        key_total[...] = jnp.zeros_like(key_total)
        value_total[...] = jnp.zeros_like(value_total)

    grad_mixed = gm_ref[...]
    prob_low = prob_ref[0]
    value_total[...] += dot_tn(prob_low, grad_mixed)
    grad_prob = dot_nt(grad_mixed, v_ref[...])
    prob = prob_low.astype(jnp.float32)
    inner = jnp.sum(grad_prob * prob, axis=-1, keepdims=True)
    score_low = (prob * (grad_prob - inner) * (1.0 / math.sqrt(HD))).astype(jnp.bfloat16)
    gq_ref[...] = turned_back(
        jnp.dot(score_low, k_ref[...], preferred_element_type=jnp.float32)
    ).astype(jnp.bfloat16)
    key_total[...] += dot_tn(score_low, q_ref[...])

    @pl.when(member == group - 1)
    def _():
        gk_ref[...] = turned_back(key_total[...]).astype(jnp.bfloat16)
        gv_ref[...] = value_total[...].astype(jnp.bfloat16)


def attention_backward(grad_mixed, query_rot, key_rot, value_low, prob_low, cos, sin):
    seq, q_width = query_rot.shape
    k_width = key_rot.shape[1]
    heads, group = q_width // HD, q_width // k_width
    per_head = pl.BlockSpec((seq, HD), lambda h: (0, h))
    per_kv = pl.BlockSpec((seq, HD), lambda h: (0, h // group))
    table = pl.BlockSpec((seq, HD), lambda h: (0, 0))
    return pl.pallas_call(
        functools.partial(backward_kernel, group),
        grid=(heads,),
        in_specs=[
            per_head,
            per_head,
            per_kv,
            per_kv,
            pl.BlockSpec((1, seq, seq), lambda h: (h, 0, 0)),
            table,
            table,
        ],
        out_specs=[per_head, per_kv, per_kv],
        out_shape=[
            jax.ShapeDtypeStruct((seq, q_width), jnp.bfloat16),
            jax.ShapeDtypeStruct((seq, k_width), jnp.bfloat16),
            jax.ShapeDtypeStruct((seq, k_width), jnp.bfloat16),
        ],
        scratch_shapes=[pltpu.VMEM((seq, HD), jnp.float32)] * 2,
        compiler_params=pltpu.CompilerParams(vmem_limit_bytes=32 * 1024 * 1024),
        cost_estimate=pl.CostEstimate(
            flops=10 * heads * seq * seq * HD,
            bytes_accessed=2 * heads * seq * seq + 6 * seq * q_width,
            transcendentals=0,
        ),
    )(grad_mixed, query_rot, key_rot, value_low, prob_low, cos, sin)


def local(
    section_inputs,
    norm_gain,
    query_weight,
    key_weight,
    value_weight,
    output_weight,
    upstream_grad,
    document_ids,
):
    pipes = lax.axis_size("pipe")
    groups = lax.axis_size("dp")
    ranks = lax.axis_size("tensor")
    section = lax.axis_index("pipe")
    sequence = lax.axis_index("dp")
    rank = lax.axis_index("tensor")
    width = section_inputs.shape[2]
    seq_len = document_ids.shape[1]
    rows = seq_len // ranks
    part = width // groups
    gain = norm_gain[0]
    w_query, w_key, w_value, w_output = (
        query_weight[0],
        key_weight[0],
        value_weight[0],
        output_weight[0],
    )
    last = pipes - 1

    def relay(block, source, target, by):
        pairs = [
            (source * ranks + i, target * ranks + (i + by) % ranks) for i in range(ranks)
        ]
        return lax.ppermute(block, ("pipe", "tensor"), pairs)

    def swap(block, by):
        return lax.ppermute(block, "dp", [(i, (i + by) % groups) for i in range(groups)])

    def columns_of(array, by):
        at = lax.rem(sequence + by, groups) * part
        return lax.dynamic_slice_in_dim(array, at, part, axis=1)

    def every_sequence(array):
        return jnp.concatenate([array] + [swap(array, by) for by in range(1, groups)], axis=0)

    def every_sequence_part(array):
        return jnp.concatenate(
            [columns_of(array, 0)] + [swap(columns_of(array, by), by) for by in range(1, groups)],
            axis=0,
        )

    def block_of(array, by):
        at = lax.rem(rank + by + ranks, ranks) * rows
        return lax.dynamic_slice_in_dim(array, at, rows, axis=0)

    cos, sin, visible = position_tables(document_ids, HD)
    inverse, unit_rows, normed_shard = normalize(section_inputs[0], gain)
    normed = lax.all_gather(normed_shard, "tensor", axis=0, tiled=True)
    query = jnp.dot(normed, w_query, preferred_element_type=jnp.float32)
    keys = jnp.dot(normed, w_key, preferred_element_type=jnp.float32)
    values = jnp.dot(normed, w_value, preferred_element_type=jnp.float32)
    query_rot, key_rot, value_low, prob_low, mixed = attention_forward(
        query, keys, values, cos, sin, visible
    )
    normed_all = every_sequence_part(normed)
    mixed_all = every_sequence(
        jnp.concatenate([block_of(mixed, -by) for by in range(ranks)], axis=0)
    )

    saved_input = None
    saved_cot = None
    saved_grads = None
    result = None
    for turn in range(pipes):
        home = last - turn
        active = section == home
        if turn == 0:
            blocks = [upstream_grad] + [
                relay(upstream_grad, home, home, by) for by in range(1, ranks)
            ]
        else:
            blocks = [relay(result, home + 1, home, by) for by in range(ranks)]
        incoming = blocks[0]
        cotangent = jnp.concatenate(blocks, axis=0)
        grad_mixed = dot_nt(cotangent, w_output).astype(jnp.bfloat16)
        grad_mixed = jnp.concatenate(
            [
                lax.dynamic_slice_in_dim(
                    grad_mixed, lax.rem(rank - b + ranks, ranks) * rows, rows, axis=0
                )
                for b in range(ranks)
            ],
            axis=0,
        )
        grads = attention_backward(grad_mixed, query_rot, key_rot, value_low, prob_low, cos, sin)

        def term(by):
            return (
                dot_nt(block_of(grads[0], by), w_query)
                + dot_nt(block_of(grads[1], by), w_key)
                + dot_nt(block_of(grads[2], by), w_value)
            ).astype(jnp.bfloat16)

        arrived = [relay(term(by), home, home, by) for by in range(1, ranks)]
        total = term(0).astype(jnp.float32)
        for one in arrived:
            total = total + one.astype(jnp.float32)
        result = back_norm(total, unit_rows, inverse, gain, incoming)
        if turn == 0:
            saved_input, saved_cot, saved_grads = result, cotangent, grads
        else:
            saved_input = jnp.where(active, result, saved_input)
            saved_cot = jnp.where(active, cotangent, saved_cot)
            saved_grads = [jnp.where(active, new, old) for new, old in zip(grads, saved_grads)]

    scale_out = 1.0 / math.sqrt(groups * seq_len)
    cot_all = every_sequence_part(saved_cot)
    output_grads = dot_tn(mixed_all, cot_all) * scale_out
    query_grads, key_grads, value_grads = [
        dot_tn(normed_all, every_sequence(one)) * scale_out for one in saved_grads
    ]
    return (
        saved_input[None],
        query_grads[None],
        key_grads[None],
        value_grads[None],
        output_grads[None],
    )


def solution(mesh):
    placed = (
        P("pipe", ("dp", "tensor"), None),
        P("pipe", None),
        P("pipe", None, "tensor"),
        P("pipe", None, "tensor"),
        P("pipe", None, "tensor"),
        P("pipe", "tensor", None),
        P(("dp", "tensor"), None),
        P("dp", None),
    )
    return jax.shard_map(
        local,
        mesh=mesh,
        in_specs=placed,
        out_specs=(
            P("pipe", ("dp", "tensor"), None),
            P("pipe", "dp", "tensor"),
            P("pipe", "dp", "tensor"),
            P("pipe", "dp", "tensor"),
            P("pipe", "tensor", "dp"),
        ),
        check_vma=False,
    )
```

time: 1260 us -> 685 us (0.54)
  waiting for transfers between devices: 1030 us -> 389 us
  matrix products: 78.4 us -> 130 us
  Pallas kernels: 0 us -> 46.7 us
  other arithmetic: 60.9 us -> 18.6 us
  starting transfers between devices: 4.66 us -> 46.6 us
  loops' own time: 28.7 us -> 0 us
    reduce_scatter x8 -> x0, waiting for transfers between devices: 625 us -> none  [the longest x4 422 us: local(): lax.psum_scatter(grad_normed, 'tensor', scatter_dimension=0, tiled=True)]
    all_gather x4 -> x0, waiting for transfers between devices: 325 us -> none  [local(): cotangent = lax.all_gather(incoming, 'tensor', axis=0, tiled=True)]
    ppermute x3 -> x33, waiting for transfers between devices: 10.2 us -> 328 us  [the longest x27 310 us: relay(): return lax.ppermute(block, ('pipe', 'tensor'), pairs)]
    dot_general x17 -> x59, matrix products: 78.4 us -> 130 us  [the longest x52 94.8 us: dot_nt(): lax.dot_general(left, right, (((1,), (1,)), ((), ())), preferred_element_...]
    pallas_call x0 -> x5, Pallas kernels: none -> 46.7 us  [the longest x4 39 us: attention_backward(): pl.pallas_call(functools.partial(backward_kernel, group), grid=(heads,),...]
    ppermute x3 -> x33, starting transfers between devices: 3.84 us -> 46.5 us  [the longest x27 40.3 us: relay(): return lax.ppermute(block, ('pipe', 'tensor'), pairs)]
    another operation x14 -> x0, local copies, waits for them, and re-layouts: 34.7 us -> none
    another operation x4 -> x0, loops' own time: 28.7 us -> none  [local(): lax.cond(active, backward_turn, skipped_turn, cotangent)]
  transfers between devices with their start and end apart: 16 -> 34, of which waited for: 15 -> 9; matrix products, arithmetic and copies ran while one was open for 7% -> 15% of each run, Pallas kernels for 0% -> 1%
where the time goes in v1:
time: 685 us; the launch traced here: 678 us
  waiting for transfers between devices  389 us (57%)
  matrix products  130 us (19%)
  Pallas kernels  46.7 us (7%)
  starting transfers between devices  46.6 us (7%)
  local copies, waits for them, and re-layouts  31.7 us (5%)
  other arithmetic  18.6 us (3%)
  between operations  16.1 us (2%)
    ppermute x27, waiting for transfers between devices, relay(): return lax.ppermute(block, ('pipe', 'tensor'), pairs)  310 us
    dot_general x52, matrix products, dot_nt(): lax.dot_general(left, right, (((1,), (1,)), ((), ())), preferred_element_...  94.8 us
    all_gather x1, waiting for transfers between devices, local(): normed = lax.all_gather(normed_shard, 'tensor', axis=0, tiled=True)  60.6 us
    ppermute x27, starting transfers between devices, relay(): return lax.ppermute(block, ('pipe', 'tensor'), pairs)  40.3 us
    pallas_call x4, Pallas kernels, attention_backward(): pl.pallas_call(functools.partial(backward_kernel, group), grid=(heads,),...  39 us
    dot_general x4, matrix products, dot_tn(): lax.dot_general(left, right, (((0,), (0,)), ((), ())), preferred_element_...  23.3 us
    unnamed x122, local copies, waits for them, and re-layouts  21.2 us
    ppermute x6, waiting for transfers between devices, swap(): lax.ppermute(block, 'dp', [(i, (i + by) % groups) for i in range(groups)])  17.9 us
  transfers between devices with their start and end apart: 34, of which 9 were waited for; matrix products, arithmetic and copies ran while one was open for 15% of the time, Pallas kernels for 1%

profile of v1, /device:TPU:8, one launch (start us, length us, event | category | flops | bytes accessed | tf_op | source)
XLA Modules:
  0.0 678.5 jit_solution(13681351771419328854)
XLA Ops:
  25.3 4.6 fusion.101
  31.0 60.6 %all-gather.2.cloned.1.call-done = bf16[512,4096]{1,0:T(8,128)(2,1)} async-done(((bf16[128,4096]{1,0:T(8,128)(2,1)}), bf16[512,4096]{1,0:T(8,128)(2,1)}) %all-gather.2.cloned.1.call-update) | async-done | bytes 4194320 | tf_op jit(solution)/shard_map/all_gather | solution.py:242
  91.6 9.4 %fusion.32.q_ref = f32[512,1024]{1,0:T(8,128)S(1)} fusion(bf16[512,4096]{1,0:T(8,128)(2,1)} %all-gather.2.cloned.1.call-done, bf16[1,4096,1024]{2,1,0:T(8,128)(2,1)} %param.10), kind=kOutput, calls=%fused_computation.32 | convolution fusion | flops 4294967296 | bytes 14680064 | tf_op jit(solution)/shard_map/dot_general | solution.py:243
  103.5 7.8 %shard_map.119 = (bf16[512,1024]{1,0:T(8,128)(2,1)S(1)}, bf16[512,128]{1,0:T(8,128)(2,1)S(1)}, bf16[512,128]{1,0:T(8,128)(2,1)S(1)}, bf16[8,512,512]{2,1,0:T(8,128)(2,1)S(1)}, bf16[512,1024]{1,0:T(8,128)(2,1)S(1)}) custom-call(f32[512,1024]{1,0:T(8,128)S(1)} %fusion.32.q_ref, f32[512,128]{1,0:T(8,128)S(1)} %fusion.157.k_ref, f32[512,128]{1,0:T(8,128)S(1)} %fusion.131.v_ref, ...), custom_call_target="tpu_custom_call" | custom-call | flops 1073741824 | bytes 8388608 | tf_op jit(solution)/shard_map/pallas_call | solution.py:93
  111.4 9.5 %shard_map.120 = (bf16[512,1024]{1,0:T(8,128)(2,1)S(1)}, bf16[512,128]{1,0:T(8,128)(2,1)S(1)}, bf16[512,128]{1,0:T(8,128)(2,1)S(1)}) custom-call(bf16[512,1024]{1,0:T(8,128)(2,1)S(1)} %copy-done.6, bf16[512,1024]{1,0:T(8,128)(2,1)S(1)} %get-tuple-element.22.q_ref, bf16[512,128]{1,0:T(8,128)(2,1)S(1)} %get-tuple-element.23.k_ref, ...), custom_call_target="tpu_custom_call" | custom-call | flops 2684354560 | bytes 7340032 | tf_op jit(solution)/shard_map/pallas_call | solution.py:157
  149.5 9.2 %fusion.104 = bf16[512,1024]{1,0:T(8,128)(2,1)S(1)} fusion(bf16[512,4096]{1,0:T(8,128)(2,1)} %constant_dynamic-update-slice_fusion.4, bf16[1,1024,4096]{2,1,0:T(8,128)(2,1)} %param.13), kind=kOutput, calls=%fused_computation.146 | convolution fusion | flops 4295491584 | bytes 13631488 | tf_op jit(solution)/shard_map/dot_general | solution.py:53
  159.7 9.7 %shard_map.121 = (bf16[512,1024]{1,0:T(8,128)(2,1)S(1)}, bf16[512,128]{1,0:T(8,128)(2,1)S(1)}, bf16[512,128]{1,0:T(8,128)(2,1)S(1)}) custom-call(bf16[512,1024]{1,0:T(8,128)(2,1)S(1)} %pad_maximum_fusion.5.gm_ref, bf16[512,1024]{1,0:T(8,128)(2,1)S(1)} %get-tuple-element.22.q_ref, bf16[512,128]{1,0:T(8,128)(2,1)S(1)} %get-tuple-element.23.k_ref, ...), custom_call_target="tpu_custom_call" | custom-call | flops 2684354560 | bytes 7340032 | tf_op jit(solution)/shard_map/pallas_call | solution.py:157
  196.8 9.2 %fusion.107 = bf16[512,1024]{1,0:T(8,128)(2,1)S(1)} fusion(bf16[512,4096]{1,0:T(8,128)(2,1)} %constant_dynamic-update-slice_fusion.8, bf16[1,1024,4096]{2,1,0:T(8,128)(2,1)} %param.13), kind=kOutput, calls=%fused_computation.147 | convolution fusion | flops 4295491584 | bytes 13631488 | tf_op jit(solution)/shard_map/dot_general | solution.py:53
  207.0 10.0 %shard_map.122 = (bf16[512,1024]{1,0:T(8,128)(2,1)S(1)}, bf16[512,128]{1,0:T(8,128)(2,1)S(1)}, bf16[512,128]{1,0:T(8,128)(2,1)S(1)}) custom-call(bf16[512,1024]{1,0:T(8,128)(2,1)S(1)} %pad_maximum_fusion.6.gm_ref, bf16[512,1024]{1,0:T(8,128)(2,1)S(1)} %get-tuple-element.22.q_ref, bf16[512,128]{1,0:T(8,128)(2,1)S(1)} %get-tuple-element.23.k_ref, ...), custom_call_target="tpu_custom_call" | custom-call | flops 2684354560 | bytes 7340032 | tf_op jit(solution)/shard_map/pallas_call | solution.py:157
  244.7 4.9 constant_dynamic-slice_fusion.7
  253.9 248.8 %collective-permute-done.20 = bf16[128,4096]{1,0:T(8,128)(2,1)} collective-permute-done((bf16[128,4096]{1,0:T(8,128)(2,1)}, bf16[128,4096]{1,0:T(8,128)(2,1)}, u32[]{:S(2)}, u32[]{:S(2)}) %collective-permute-start.20) | collective-permute-done | bytes 1048608 | tf_op jit(solution)/shard_map/ppermute | solution.py:218
  506.1 13.8 %collective-permute-done.22 = bf16[128,4096]{1,0:T(8,128)(2,1)S(1)} collective-permute-done((bf16[128,4096]{1,0:T(8,128)(2,1)}, bf16[128,4096]{1,0:T(8,128)(2,1)S(1)}, u32[]{:S(2)}, u32[]{:S(2)}) %collective-permute-start.22) | collective-permute-done | bytes 1048608 | tf_op jit(solution)/shard_map/ppermute | solution.py:218
  520.0 22.3 %collective-permute-done.23 = bf16[128,4096]{1,0:T(8,128)(2,1)S(1)} collective-permute-done((bf16[128,4096]{1,0:T(8,128)(2,1)}, bf16[128,4096]{1,0:T(8,128)(2,1)S(1)}, u32[]{:S(2)}, u32[]{:S(2)}) %collective-permute-start.23) | collective-permute-done | bytes 1048608 | tf_op jit(solution)/shard_map/ppermute | solution.py:218
  542.4 7.2 %fusion.110 = bf16[512,1024]{1,0:T(8,128)(2,1)S(1)} fusion(bf16[512,4096]{1,0:T(8,128)(2,1)S(1)} %constant_dynamic-update-slice_fusion.12, bf16[1,1024,4096]{2,1,0:T(8,128)(2,1)} %param.13), kind=kOutput, calls=%fused_computation.148 | convolution fusion | flops 4295491584 | bytes 13631488 | tf_op jit(solution)/shard_map/dot_general | solution.py:53
  551.0 9.7 %shard_map.123 = (bf16[512,1024]{1,0:T(8,128)(2,1)S(1)}, bf16[512,128]{1,0:T(8,128)(2,1)S(1)}, bf16[512,128]{1,0:T(8,128)(2,1)S(1)}) custom-call(bf16[512,1024]{1,0:T(8,128)(2,1)S(1)} %pad_maximum_fusion.7.gm_ref, bf16[512,1024]{1,0:T(8,128)(2,1)S(1)} %copy-done.20, bf16[512,128]{1,0:T(8,128)(2,1)S(1)} %copy-done.22, bf16[512,128]{1,0:T(8,128)(2,1)S(1)} %copy-done.24, ...), custom_call_target="tpu_custom_call" | custom-call | flops 2684354560 | bytes 7340032 | tf_op jit(solution)/shard_map/pallas_call | solution.py:157
  578.9 11.0 %collective-permute-start.25 = (bf16[128,4096]{1,0:T(8,128)(2,1)S(1)}, bf16[128,4096]{1,0:T(8,128)(2,1)S(1)}, u32[]{:S(2)}, u32[]{:S(2)}) collective-permute-start(bf16[128,4096]{1,0:T(8,128)(2,1)S(1)} %fusion.60), channel_id=1, source_target_pairs={{0,2},{1,3},{2,0},{3,1},{4,6},{5,7},{6,4},{7,5}} | collective-permute-start | bytes 3145736 | tf_op jit(solution)/shard_map/ppermute | solution.py:218
  590.9 4.2 collective-permute-start.26
  600.3 3.9 fusion.74
  605.0 3.9 fusion.75
  608.9 15.9 %collective-permute-done.25 = bf16[128,4096]{1,0:T(8,128)(2,1)S(1)} collective-permute-done((bf16[128,4096]{1,0:T(8,128)(2,1)S(1)}, bf16[128,4096]{1,0:T(8,128)(2,1)S(1)}, u32[]{:S(2)}, u32[]{:S(2)}) %collective-permute-start.25) | collective-permute-done | bytes 1048608 | tf_op jit(solution)/shard_map/ppermute | solution.py:218
  624.8 8.9 %collective-permute-done.26 = bf16[128,4096]{1,0:T(8,128)(2,1)S(1)} collective-permute-done((bf16[128,4096]{1,0:T(8,128)(2,1)S(1)}, bf16[128,4096]{1,0:T(8,128)(2,1)S(1)}, u32[]{:S(2)}, u32[]{:S(2)}) %collective-permute-start.26) | collective-permute-done | bytes 1048608 | tf_op jit(solution)/shard_map/ppermute | solution.py:218
  634.9 8.6 %multiply_bitcast_fusion.1 = f32[1,2048,1024]{2,1,0:T(8,128)} fusion(bf16[512,1024]{1,0:T(8,128)(2,1)S(1)} %collective-permute-done.28, bf16[512,1024]{1,0:T(8,128)(2,1)S(1)} %select_select_fusion.1, bf16[512,2048]{1,0:T(8,128)(2,1)} %collective-permute-done.27, bf16[512,2048]{1,0:T(8,128)(2,1)S(1)} %copy-done.40), kind=kOutput, calls=%fused_computation.43 | convolution fusion | flops 4309647360 | bytes 14680064 | tf_op jit(solution)/shard_map/dot_general | solution.py:59
  646.9 17.4 %collective-permute-done.32 = bf16[512,2048]{1,0:T(8,128)(2,1)S(1)} collective-permute-done((bf16[512,2048]{1,0:T(8,128)(2,1)S(1)}, bf16[512,2048]{1,0:T(8,128)(2,1)S(1)}, u32[]{:S(2)}, u32[]{:S(2)}) %collective-permute-start.32) | collective-permute-done | bytes 2097184 | tf_op jit(solution)/shard_map/ppermute | solution.py:221
  664.3 6.9 %multiply_bitcast_fusion = f32[1,1024,2048]{2,1,0:T(8,128)} fusion(bf16[1024,1024]{1,0:T(8,128)(2,1)S(1)} %copy-done.47, bf16[512,2048]{1,0:T(8,128)(2,1)S(1)} %collective-permute-done.32, bf16[512,2048]{1,0:T(8,128)(2,1)S(1)} %get-tuple-element.47), kind=kOutput, calls=%fused_computation.42 | convolution fusion | flops 4305453056 | bytes 14680064 | tf_op jit(solution)/shard_map/dot_general | solution.py:59
  (271 shorter events, 145.1 us)
Async XLA Ops:
  7.2 84.4 %all-gather.2.cloned.1.call-start = ((), (), s32[]{:S(2)}) async-start(), calls=%async_computation | async-start | bytes 5242880 | tf_op jit(solution)/shard_map/all_gather | solution.py:242
  12.1 8.2 %collective-permute-start = (bf16[128,4096]{1,0:T(8,128)(2,1)}, bf16[128,4096]{1,0:T(8,128)(2,1)}, u32[]{:S(2)}, u32[]{:S(2)}) collective-permute-start(bf16[128,4096]{1,0:T(8,128)(2,1)} %param.14), channel_id=1, source_target_pairs={{24,25},{25,26},{26,27},{27,24},{28,29},{29,30},{30,31},{31,28}} | collective-permute-start | bytes 3145736 | tf_op jit(solution)/shard_map/ppermute | solution.py:218
  13.8 8.8 %collective-permute-start.1 = (bf16[128,4096]{1,0:T(8,128)(2,1)}, bf16[128,4096]{1,0:T(8,128)(2,1)}, u32[]{:S(2)}, u32[]{:S(2)}) collective-permute-start(bf16[128,4096]{1,0:T(8,128)(2,1)} %param.14), channel_id=1, source_target_pairs={{24,26},{25,27},{26,24},{27,25},{28,30},{29,31},{30,28},{31,29}} | collective-permute-start | bytes 3145736 | tf_op jit(solution)/shard_map/ppermute | solution.py:218
  15.4 8.5 %collective-permute-start.2 = (bf16[128,4096]{1,0:T(8,128)(2,1)}, bf16[128,4096]{1,0:T(8,128)(2,1)}, u32[]{:S(2)}, u32[]{:S(2)}) collective-permute-start(bf16[128,4096]{1,0:T(8,128)(2,1)} %param.14), channel_id=1, source_target_pairs={{24,27},{25,24},{26,25},{27,26},{28,31},{29,28},{30,29},{31,30}} | collective-permute-start | bytes 3145736 | tf_op jit(solution)/shard_map/ppermute | solution.py:218
  124.8 13.6 %collective-permute-start.3 = (bf16[128,4096]{1,0:T(8,128)(2,1)S(1)}, bf16[128,4096]{1,0:T(8,128)(2,1)S(1)}, u32[]{:S(2)}, u32[]{:S(2)}) collective-permute-start(bf16[128,4096]{1,0:T(8,128)(2,1)S(1)} %fusion.44), channel_id=1, source_target_pairs={{24,25},{25,26},{26,27},{27,24},{28,29},{29,30},{30,31},{31,28}} | collective-permute-start | bytes 3145736 | tf_op jit(solution)/shard_map/ppermute | solution.py:218
  129.3 9.1 %collective-permute-start.4 = (bf16[128,4096]{1,0:T(8,128)(2,1)S(1)}, bf16[128,4096]{1,0:T(8,128)(2,1)S(1)}, u32[]{:S(2)}, u32[]{:S(2)}) collective-permute-start(bf16[128,4096]{1,0:T(8,128)(2,1)S(1)} %fusion.45), channel_id=1, source_target_pairs={{24,26},{25,27},{26,24},{27,25},{28,30},{29,31},{30,28},{31,29}} | collective-permute-start | bytes 3145736 | tf_op jit(solution)/shard_map/ppermute | solution.py:218
  179.1 8.6 %collective-permute-start.10 = (bf16[128,4096]{1,0:T(8,128)(2,1)S(1)}, bf16[128,4096]{1,0:T(8,128)(2,1)S(1)}, u32[]{:S(2)}, u32[]{:S(2)}) collective-permute-start(bf16[128,4096]{1,0:T(8,128)(2,1)S(1)} %fusion.49), channel_id=1, source_target_pairs={{16,17},{17,18},{18,19},{19,16},{20,21},{21,22},{22,23},{23,20}} | collective-permute-start | bytes 3145736 | tf_op jit(solution)/shard_map/ppermute | solution.py:218
  180.7 6.9 %collective-permute-start.11 = (bf16[128,4096]{1,0:T(8,128)(2,1)S(1)}, bf16[128,4096]{1,0:T(8,128)(2,1)S(1)}, u32[]{:S(2)}, u32[]{:S(2)}) collective-permute-start(bf16[128,4096]{1,0:T(8,128)(2,1)S(1)} %fusion.50), channel_id=1, source_target_pairs={{16,18},{17,19},{18,16},{19,17},{20,22},{21,23},{22,20},{23,21}} | collective-permute-start | bytes 3145736 | tf_op jit(solution)/shard_map/ppermute | solution.py:218
  226.6 12.5 %collective-permute-start.17 = (bf16[128,4096]{1,0:T(8,128)(2,1)S(1)}, bf16[128,4096]{1,0:T(8,128)(2,1)S(1)}, u32[]{:S(2)}, u32[]{:S(2)}) collective-permute-start(bf16[128,4096]{1,0:T(8,128)(2,1)S(1)} %fusion.54), channel_id=1, source_target_pairs={{8,9},{9,10},{10,11},{11,8},{12,13},{13,14},{14,15},{15,12}} | collective-permute-start | bytes 3145736 | tf_op jit(solution)/shard_map/ppermute | solution.py:218
  228.3 10.9 %collective-permute-start.18 = (bf16[128,4096]{1,0:T(8,128)(2,1)S(1)}, bf16[128,4096]{1,0:T(8,128)(2,1)S(1)}, u32[]{:S(2)}, u32[]{:S(2)}) collective-permute-start(bf16[128,4096]{1,0:T(8,128)(2,1)S(1)} %fusion.55), channel_id=1, source_target_pairs={{8,10},{9,11},{10,8},{11,9},{12,14},{13,15},{14,12},{15,13}} | collective-permute-start | bytes 3145736 | tf_op jit(solution)/shard_map/ppermute | solution.py:218
  229.9 9.3 %collective-permute-start.19 = (bf16[128,4096]{1,0:T(8,128)(2,1)S(1)}, bf16[128,4096]{1,0:T(8,128)(2,1)S(1)}, u32[]{:S(2)}, u32[]{:S(2)}) collective-permute-start(bf16[128,4096]{1,0:T(8,128)(2,1)S(1)} %fusion.56), channel_id=1, source_target_pairs={{8,11},{9,8},{10,9},{11,10},{12,15},{13,12},{14,13},{15,14}} | collective-permute-start | bytes 3145736 | tf_op jit(solution)/shard_map/ppermute | solution.py:218
  234.1 17.1 %collective-permute-start.31 = (bf16[512,1024]{1,0:T(8,128)(2,1)}, bf16[512,1024]{1,0:T(8,128)(2,1)}, u32[]{:S(2)}, u32[]{:S(2)}) collective-permute-start(bf16[512,1024]{1,0:T(8,128)(2,1)} %pad_maximum_fusion.8), channel_id=1, source_target_pairs={{0,4},{4,0},{1,5},{5,1},{2,6},{6,2},{3,7},{7,3},{8,12},{12,8},{9,1... | collective-permute-start | bytes 3145736 | tf_op jit(solution)/shard_map/ppermute | solution.py:221
  242.1 260.6 %collective-permute-start.20 = (bf16[128,4096]{1,0:T(8,128)(2,1)}, bf16[128,4096]{1,0:T(8,128)(2,1)}, u32[]{:S(2)}, u32[]{:S(2)}) collective-permute-start(bf16[128,4096]{1,0:T(8,128)(2,1)} %fusion.91), channel_id=1, source_target_pairs={{8,0},{9,1},{10,2},{11,3},{12,4},{13,5},{14,6},{15,7}} | collective-permute-start | bytes 3145736 | tf_op jit(solution)/shard_map/ppermute | solution.py:218
  243.4 261.3 %collective-permute-start.21 = (bf16[128,4096]{1,0:T(8,128)(2,1)}, bf16[128,4096]{1,0:T(8,128)(2,1)}, u32[]{:S(2)}, u32[]{:S(2)}) collective-permute-start(bf16[128,4096]{1,0:T(8,128)(2,1)} %fusion.91), channel_id=1, source_target_pairs={{8,1},{9,2},{10,3},{11,0},{12,5},{13,6},{14,7},{15,4}} | collective-permute-start | bytes 3145736 | tf_op jit(solution)/shard_map/ppermute | solution.py:218
  249.6 348.5 %collective-permute-start.27 = (bf16[512,2048]{1,0:T(8,128)(2,1)}, bf16[512,2048]{1,0:T(8,128)(2,1)}, u32[]{:S(2)}, u32[]{:S(2)}) collective-permute-start(bf16[512,2048]{1,0:T(8,128)(2,1)} %get-tuple-element.50), channel_id=1, source_target_pairs={{0,4},{4,0},{1,5},{5,1},{2,6},{6,2},{3,7},{7,3},{8,12},{12,8},{9,1... | collective-permute-start | bytes 6291464 | tf_op jit(solution)/shard_map/ppermute | solution.py:221
  250.0 269.9 %collective-permute-start.22 = (bf16[128,4096]{1,0:T(8,128)(2,1)}, bf16[128,4096]{1,0:T(8,128)(2,1)S(1)}, u32[]{:S(2)}, u32[]{:S(2)}) collective-permute-start(bf16[128,4096]{1,0:T(8,128)(2,1)} %fusion.91), channel_id=1, source_target_pairs={{8,2},{9,3},{10,0},{11,1},{12,6},{13,7},{14,4},{15,5}} | collective-permute-start | bytes 3145736 | tf_op jit(solution)/shard_map/ppermute | solution.py:218
  251.3 291.1 %collective-permute-start.23 = (bf16[128,4096]{1,0:T(8,128)(2,1)}, bf16[128,4096]{1,0:T(8,128)(2,1)S(1)}, u32[]{:S(2)}, u32[]{:S(2)}) collective-permute-start(bf16[128,4096]{1,0:T(8,128)(2,1)} %fusion.91), channel_id=1, source_target_pairs={{8,3},{9,0},{10,1},{11,2},{12,7},{13,4},{14,5},{15,6}} | collective-permute-start | bytes 3145736 | tf_op jit(solution)/shard_map/ppermute | solution.py:218
  573.5 25.2 %collective-permute-start.30 = (bf16[512,128]{1,0:T(8,128)(2,1)S(1)}, bf16[512,128]{1,0:T(8,128)(2,1)S(1)}, u32[]{:S(2)}, u32[]{:S(2)}) collective-permute-start(bf16[512,128]{1,0:T(8,128)(2,1)S(1)} %select_select_fusion.2), channel_id=1, source_target_pairs={{0,4},{4,0},{1,5},{5,1},{2,6},{6,2},{3,7},{7,3},{8,12},{12,8},{9,1... | collective-permute-start | bytes 393224 | tf_op jit(solution)/shard_map/ppermute | solution.py:221
  576.1 32.8 %collective-permute-start.24 = (bf16[128,4096]{1,0:T(8,128)(2,1)S(1)}, bf16[128,4096]{1,0:T(8,128)(2,1)S(1)}, u32[]{:S(2)}, u32[]{:S(2)}) collective-permute-start(bf16[128,4096]{1,0:T(8,128)(2,1)S(1)} %fusion.59), channel_id=1, source_target_pairs={{0,1},{1,2},{2,3},{3,0},{4,5},{5,6},{6,7},{7,4}} | collective-permute-start | bytes 3145736 | tf_op jit(solution)/shard_map/ppermute | solution.py:218
  578.9 45.8 %collective-permute-start.25 = (bf16[128,4096]{1,0:T(8,128)(2,1)S(1)}, bf16[128,4096]{1,0:T(8,128)(2,1)S(1)}, u32[]{:S(2)}, u32[]{:S(2)}) collective-permute-start(bf16[128,4096]{1,0:T(8,128)(2,1)S(1)} %fusion.60), channel_id=1, source_target_pairs={{0,2},{1,3},{2,0},{3,1},{4,6},{5,7},{6,4},{7,5}} | collective-permute-start | bytes 3145736 | tf_op jit(solution)/shard_map/ppermute | solution.py:218
  590.9 42.7 %collective-permute-start.26 = (bf16[128,4096]{1,0:T(8,128)(2,1)S(1)}, bf16[128,4096]{1,0:T(8,128)(2,1)S(1)}, u32[]{:S(2)}, u32[]{:S(2)}) collective-permute-start(bf16[128,4096]{1,0:T(8,128)(2,1)S(1)} %fusion.61), channel_id=1, source_target_pairs={{0,3},{1,0},{2,1},{3,2},{4,7},{5,4},{6,5},{7,6}} | collective-permute-start | bytes 3145736 | tf_op jit(solution)/shard_map/ppermute | solution.py:218
  598.2 6.5 collective-permute-start.29
  598.6 36.2 %collective-permute-start.28 = (bf16[512,1024]{1,0:T(8,128)(2,1)S(1)}, bf16[512,1024]{1,0:T(8,128)(2,1)S(1)}, u32[]{:S(2)}, u32[]{:S(2)}) collective-permute-start(bf16[512,1024]{1,0:T(8,128)(2,1)S(1)} %select_select_fusion.1), channel_id=1, source_target_pairs={{0,4},{4,0},{1,5},{5,1},{2,6},{6,2},{3,7},{7,3},{8,12},{12,8},{9,1... | collective-permute-start | bytes 3145736 | tf_op jit(solution)/shard_map/ppermute | solution.py:221
  604.7 59.6 %collective-permute-start.32 = (bf16[512,2048]{1,0:T(8,128)(2,1)S(1)}, bf16[512,2048]{1,0:T(8,128)(2,1)S(1)}, u32[]{:S(2)}, u32[]{:S(2)}) collective-permute-start(bf16[512,2048]{1,0:T(8,128)(2,1)S(1)} %get-tuple-element.48), channel_id=1, source_target_pairs={{0,4},{4,0},{1,5},{5,1},{2,6},{6,2},{3,7},{7,3},{8,12},{12,8},{9,1... | collective-permute-start | bytes 6291464 | tf_op jit(solution)/shard_map/ppermute | solution.py:221
  (63 other events, 1279.7 us)
Sparse Core Ops, SparseCore 0:
  12.3 79.2 all-gather.1

commit v2 on v1

--- a/solution.py
+++ b/solution.py
@@ -210,6 +210,7 @@
         output_weight[0],
     )
     last = pipes - 1
+    scale_out = 1.0 / math.sqrt(groups * seq_len)
 
     def relay(block, source, target, by):
         pairs = [
@@ -217,6 +218,23 @@
         ]
         return lax.ppermute(block, ("pipe", "tensor"), pairs)
 
+    def relay_within(block, sections, by):
+        pairs = [
+            (p * ranks + i, p * ranks + (i + by) % ranks) for p in sections for i in range(ranks)
+        ]
+        return lax.ppermute(block, ("pipe", "tensor"), pairs)
+
+    def natural(array):
+        return jnp.concatenate(
+            [
+                lax.dynamic_slice_in_dim(
+                    array, lax.rem(rank - b + ranks, ranks) * rows, rows, axis=0
+                )
+                for b in range(ranks)
+            ],
+            axis=0,
+        )
+
     def swap(block, by):
         return lax.ppermute(block, "dp", [(i, (i + by) % groups) for i in range(groups)])
 
@@ -239,44 +257,51 @@
 
     cos, sin, visible = position_tables(document_ids, HD)
     inverse, unit_rows, normed_shard = normalize(section_inputs[0], gain)
-    normed = lax.all_gather(normed_shard, "tensor", axis=0, tiled=True)
-    query = jnp.dot(normed, w_query, preferred_element_type=jnp.float32)
-    keys = jnp.dot(normed, w_key, preferred_element_type=jnp.float32)
-    values = jnp.dot(normed, w_value, preferred_element_type=jnp.float32)
+    early = [p for p in range(pipes) if (last - p) % 2 == 0]
+    late = [p for p in range(pipes) if (last - p) % 2 == 1]
+    first = [relay_within(normed_shard, early, by) for by in range(1, ranks)]
+    upstream = [upstream_grad] + [
+        relay(upstream_grad, last, last, by) for by in range(1, ranks)
+    ]
+    seen = sum(one[:8, :128].astype(jnp.float32) for one in first + upstream[1:])
+    pairs = [((p + 1) * ranks + i, p * ranks + i) for p in late for i in range(ranks)]
+    seen = lax.ppermute(seen, ("pipe", "tensor"), pairs)
+    waiting = normed_shard + (seen[0, 0] * 0.0).astype(jnp.bfloat16)
+    second = [relay_within(waiting, late, by) for by in range(1, ranks)]
+    is_early = lax.rem(last - section, 2) == 0
+    held = jnp.concatenate(
+        [normed_shard] + [jnp.where(is_early, x, y) for x, y in zip(first, second)], axis=0
+    )
+    query = natural(jnp.dot(held, w_query, preferred_element_type=jnp.float32))
+    keys = natural(jnp.dot(held, w_key, preferred_element_type=jnp.float32))
+    values = natural(jnp.dot(held, w_value, preferred_element_type=jnp.float32))
     query_rot, key_rot, value_low, prob_low, mixed = attention_forward(
         query, keys, values, cos, sin, visible
     )
-    normed_all = every_sequence_part(normed)
+    normed_all = every_sequence_part(natural(held))
     mixed_all = every_sequence(
         jnp.concatenate([block_of(mixed, -by) for by in range(ranks)], axis=0)
     )
 
-    saved_input = None
-    saved_cot = None
-    saved_grads = None
-    result = None
     for turn in range(pipes):
         home = last - turn
         active = section == home
         if turn == 0:
-            blocks = [upstream_grad] + [
-                relay(upstream_grad, home, home, by) for by in range(1, ranks)
-            ]
+            blocks = upstream
         else:
             blocks = [relay(result, home + 1, home, by) for by in range(ranks)]
         incoming = blocks[0]
         cotangent = jnp.concatenate(blocks, axis=0)
         grad_mixed = dot_nt(cotangent, w_output).astype(jnp.bfloat16)
-        grad_mixed = jnp.concatenate(
-            [
-                lax.dynamic_slice_in_dim(
-                    grad_mixed, lax.rem(rank - b + ranks, ranks) * rows, rows, axis=0
-                )
-                for b in range(ranks)
-            ],
-            axis=0,
-        )
+        grad_mixed = natural(grad_mixed)
         grads = attention_backward(grad_mixed, query_rot, key_rot, value_low, prob_low, cos, sin)
+        if turn == 0:
+            saved_cot, saved_grads = cotangent, grads
+        else:
+            saved_cot = jnp.where(active, cotangent, saved_cot)
+            saved_grads = [jnp.where(active, new, old) for new, old in zip(grads, saved_grads)]
+        if turn == last:
+            cot_all = every_sequence_part(saved_cot)
 
         def term(by):
             return (
@@ -285,24 +310,26 @@
                 + dot_nt(block_of(grads[2], by), w_value)
             ).astype(jnp.bfloat16)
 
-        arrived = [relay(term(by), home, home, by) for by in range(1, ranks)]
-        total = term(0).astype(jnp.float32)
+        sent = [term(by) for by in range(1, ranks)]
+        arrived = [relay(one, home, home, by) for by, one in enumerate(sent, 1)]
+        own = term(0)
+        if turn == last:
+            normed_all, mixed_all, sent, own = lax.optimization_barrier(
+                (normed_all, mixed_all, sent, own)
+            )
+            output_grads = dot_tn(mixed_all, cot_all) * scale_out
+            query_grads, key_grads, value_grads = [
+                dot_tn(normed_all, every_sequence(one)) * scale_out for one in saved_grads
+            ]
+            own, output_grads, query_grads, key_grads, value_grads = lax.optimization_barrier(
+                (own, output_grads, query_grads, key_grads, value_grads)
+            )
+        total = own.astype(jnp.float32)
         for one in arrived:
             total = total + one.astype(jnp.float32)
         result = back_norm(total, unit_rows, inverse, gain, incoming)
-        if turn == 0:
-            saved_input, saved_cot, saved_grads = result, cotangent, grads
-        else:
-            saved_input = jnp.where(active, result, saved_input)
-            saved_cot = jnp.where(active, cotangent, saved_cot)
-            saved_grads = [jnp.where(active, new, old) for new, old in zip(grads, saved_grads)]
-
-    scale_out = 1.0 / math.sqrt(groups * seq_len)
-    cot_all = every_sequence_part(saved_cot)
-    output_grads = dot_tn(mixed_all, cot_all) * scale_out
-    query_grads, key_grads, value_grads = [
-        dot_tn(normed_all, every_sequence(one)) * scale_out for one in saved_grads
-    ]
+        saved_input = result if turn == 0 else jnp.where(active, result, saved_input)
+
     return (
         saved_input[None],
         query_grads[None],

time: 685 us -> 676 us (0.987)
  waiting for transfers between devices: 389 us -> 357 us
  starting transfers between devices: 46.6 us -> 64.8 us
  between operations: 16.1 us -> 3.64 us
  other arithmetic: 18.6 us -> 25.7 us
    ppermute x27, waiting for transfers between devices: 310 us -> 234 us  [relay(): return lax.ppermute(block, ('pipe', 'tensor'), pairs)]
    ppermute x0 -> x7, waiting for transfers between devices: none -> 70.8 us  [the longest x1 37.9 us: local(): seen = lax.ppermute(seen, ('pipe', 'tensor'), pairs)]
    all_gather x1 -> x0, waiting for transfers between devices: 60.6 us -> none  [local(): normed = lax.all_gather(normed_shard, 'tensor', axis=0, tiled=True)]
    ppermute x6, waiting for transfers between devices: 17.9 us -> 51.5 us  [swap(): lax.ppermute(block, 'dp', [(i, (i + by) % groups) for i in range(groups)])]
    ppermute x0 -> x7, starting transfers between devices: none -> 16 us  [the longest x6 14.7 us: relay_within(): return lax.ppermute(block, ('pipe', 'tensor'), pairs)]
    dot_general x52, matrix products: 94.8 us -> 109 us  [dot_nt(): lax.dot_general(left, right, (((1,), (1,)), ((), ())), preferred_element_...]
    unnamed x122 -> x144, local copies, waits for them, and re-layouts: 21.2 us -> 25.7 us
  transfers between devices with their start and end apart: 34 -> 40, of which waited for: 9 -> 8; matrix products, arithmetic and copies ran while one was open for 15% -> 17% of each run, Pallas kernels for 1% -> 1%
where the time goes in v2:
time: 676 us; the launch traced here: 667 us
  waiting for transfers between devices  357 us (53%)
  matrix products  135 us (20%)
  starting transfers between devices  64.8 us (10%)
  Pallas kernels  46.3 us (7%)
  local copies, waits for them, and re-layouts  34.8 us (5%)
  other arithmetic  25.7 us (4%)
    ppermute x27, waiting for transfers between devices, relay(): return lax.ppermute(block, ('pipe', 'tensor'), pairs)  234 us
    dot_general x52, matrix products, dot_nt(): lax.dot_general(left, right, (((1,), (1,)), ((), ())), preferred_element_...  109 us
    ppermute x6, waiting for transfers between devices, swap(): lax.ppermute(block, 'dp', [(i, (i + by) % groups) for i in range(groups)])  51.5 us
    ppermute x27, starting transfers between devices, relay(): return lax.ppermute(block, ('pipe', 'tensor'), pairs)  42.5 us
    pallas_call x4, Pallas kernels, attention_backward(): pl.pallas_call(functools.partial(backward_kernel, group), grid=(heads,),...  38.4 us
    ppermute x1, waiting for transfers between devices, local(): seen = lax.ppermute(seen, ('pipe', 'tensor'), pairs)  37.9 us
    ppermute x6, waiting for transfers between devices, relay_within(): return lax.ppermute(block, ('pipe', 'tensor'), pairs)  32.9 us
    unnamed x144, local copies, waits for them, and re-layouts  25.7 us
  transfers between devices with their start and end apart: 40, of which 8 were waited for; matrix products, arithmetic and copies ran while one was open for 17% of the time, Pallas kernels for 1%

profile of v2, /device:TPU:8, one launch (start us, length us, event | category | flops | bytes accessed | tf_op | source)
XLA Modules:
  0.0 666.9 jit_solution(3552148933582146086)
XLA Ops:
  24.5 37.9 %collective-permute-done.6 = f32[8,128]{1,0:T(8,128)S(1)} collective-permute-done((f32[8,128]{1,0:T(8,128)S(1)}, f32[8,128]{1,0:T(8,128)S(1)}, u32[]{:S(2)}, u32[]{:S(2)}) %collective-permute-start.6) | collective-permute-done | bytes 4128 | tf_op jit(solution)/shard_map/ppermute | solution.py:268
  65.9 7.1 %fusion.98 = bf16[512,1024]{1,0:T(8,128)(2,1)S(1)} fusion(bf16[512,4096]{1,0:T(8,128)(2,1)S(1)} %constant_dynamic-update-slice_fusion, bf16[1,1024,4096]{2,1,0:T(8,128)(2,1)} %param.13), kind=kOutput, calls=%fused_computation.145 | convolution fusion | flops 4295491584 | bytes 13631488 | tf_op jit(solution)/shard_map/dot_general | solution.py:53
  76.7 4.1 collective-permute-start.9
  81.0 31.0 %collective-permute-done.8 = bf16[128,4096]{1,0:T(8,128)(2,1)S(1)} collective-permute-done((bf16[128,4096]{1,0:T(8,128)(2,1)S(1)}, bf16[128,4096]{1,0:T(8,128)(2,1)S(1)}, u32[]{:S(2)}, u32[]{:S(2)}) %collective-permute-start.8) | collective-permute-done | bytes 1048608 | tf_op jit(solution)/shard_map/ppermute | solution.py:225
  119.4 4.6 fusion.32
  124.4 7.9 %shard_map.119 = (bf16[512,1024]{1,0:T(8,128)(2,1)S(1)}, bf16[512,128]{1,0:T(8,128)(2,1)S(1)}, bf16[512,128]{1,0:T(8,128)(2,1)S(1)}, bf16[8,512,512]{2,1,0:T(8,128)(2,1)S(1)}, bf16[512,1024]{1,0:T(8,128)(2,1)S(1)}) custom-call(f32[512,1024]{1,0:T(8,128)S(1)} %pad_maximum_fusion.3.q_ref, f32[512,128]{1,0:T(8,128)S(1)} %pad_maximum_fusion.9.k_ref, ...), custom_call_target="tpu_custom_call" | custom-call | flops 1073741824 | bytes 8388608 | tf_op jit(solution)/shard_map/pallas_call | solution.py:93
  133.3 9.6 %shard_map.120 = (bf16[512,1024]{1,0:T(8,128)(2,1)S(1)}, bf16[512,128]{1,0:T(8,128)(2,1)S(1)}, bf16[512,128]{1,0:T(8,128)(2,1)S(1)}) custom-call(bf16[512,1024]{1,0:T(8,128)(2,1)S(1)} %pad_maximum_fusion.4.gm_ref, bf16[512,1024]{1,0:T(8,128)(2,1)S(1)} %get-tuple-element.30.q_ref, bf16[512,128]{1,0:T(8,128)(2,1)S(1)} %get-tuple-element.31.k_ref, ...), custom_call_target="tpu_custom_call" | custom-call | flops 2684354560 | bytes 7340032 | tf_op jit(solution)/shard_map/pallas_call | solution.py:157
  169.9 9.2 %fusion.101 = bf16[512,1024]{1,0:T(8,128)(2,1)S(1)} fusion(bf16[512,4096]{1,0:T(8,128)(2,1)} %constant_dynamic-update-slice_fusion.4, bf16[1,1024,4096]{2,1,0:T(8,128)(2,1)} %param.13), kind=kOutput, calls=%fused_computation.146 | convolution fusion | flops 4295491584 | bytes 13631488 | tf_op jit(solution)/shard_map/dot_general | solution.py:53
  179.3 9.6 %shard_map.121 = (bf16[512,1024]{1,0:T(8,128)(2,1)S(1)}, bf16[512,128]{1,0:T(8,128)(2,1)S(1)}, bf16[512,128]{1,0:T(8,128)(2,1)S(1)}) custom-call(bf16[512,1024]{1,0:T(8,128)(2,1)S(1)} %pad_maximum_fusion.5.gm_ref, bf16[512,1024]{1,0:T(8,128)(2,1)S(1)} %get-tuple-element.30.q_ref, bf16[512,128]{1,0:T(8,128)(2,1)S(1)} %get-tuple-element.31.k_ref, ...), custom_call_target="tpu_custom_call" | custom-call | flops 2684354560 | bytes 7340032 | tf_op jit(solution)/shard_map/pallas_call | solution.py:157
  208.6 6.3 fusion.22
  229.7 8.9 %fusion.104 = bf16[512,1024]{1,0:T(8,128)(2,1)S(1)} fusion(bf16[512,4096]{1,0:T(8,128)(2,1)S(1)} %constant_dynamic-update-slice_fusion.8, bf16[1,1024,4096]{2,1,0:T(8,128)(2,1)} %param.13), kind=kOutput, calls=%fused_computation.147 | convolution fusion | flops 4295491584 | bytes 13631488 | tf_op jit(solution)/shard_map/dot_general | solution.py:53
  241.0 9.5 %shard_map.122 = (bf16[512,1024]{1,0:T(8,128)(2,1)S(1)}, bf16[512,128]{1,0:T(8,128)(2,1)S(1)}, bf16[512,128]{1,0:T(8,128)(2,1)S(1)}) custom-call(bf16[512,1024]{1,0:T(8,128)(2,1)S(1)} %pad_maximum_fusion.6.gm_ref, bf16[512,1024]{1,0:T(8,128)(2,1)S(1)} %copy-done.22, bf16[512,128]{1,0:T(8,128)(2,1)S(1)} %copy-done.25, bf16[512,128]{1,0:T(8,128)(2,1)S(1)} %copy-done.28, ...), custom_call_target="tpu_custom_call" | custom-call | flops 2684354560 | bytes 7340032 | tf_op jit(solution)/shard_map/pallas_call | solution.py:157
  284.1 200.6 %collective-permute-done.27 = bf16[128,4096]{1,0:T(8,128)(2,1)} collective-permute-done((bf16[128,4096]{1,0:T(8,128)(2,1)}, bf16[128,4096]{1,0:T(8,128)(2,1)}, u32[]{:S(2)}, u32[]{:S(2)}) %collective-permute-start.27) | collective-permute-done | bytes 1048608 | tf_op jit(solution)/shard_map/ppermute | solution.py:219
  489.4 12.6 %collective-permute-done.31 = bf16[128,4096]{1,0:T(8,128)(2,1)S(1)} collective-permute-done((bf16[128,4096]{1,0:T(8,128)(2,1)}, bf16[128,4096]{1,0:T(8,128)(2,1)S(1)}, u32[]{:S(2)}, u32[]{:S(2)}) %collective-permute-start.31) | collective-permute-done | bytes 1048608 | tf_op jit(solution)/shard_map/ppermute | solution.py:219
  503.0 21.3 %collective-permute-done.32 = bf16[128,4096]{1,0:T(8,128)(2,1)S(1)} collective-permute-done((bf16[128,4096]{1,0:T(8,128)(2,1)}, bf16[128,4096]{1,0:T(8,128)(2,1)S(1)}, u32[]{:S(2)}, u32[]{:S(2)}) %collective-permute-start.32) | collective-permute-done | bytes 1048608 | tf_op jit(solution)/shard_map/ppermute | solution.py:219
  525.4 9.3 %fusion.107 = bf16[512,1024]{1,0:T(8,128)(2,1)S(1)} fusion(bf16[512,4096]{1,0:T(8,128)(2,1)} %constant_dynamic-update-slice_fusion.17, bf16[1,1024,4096]{2,1,0:T(8,128)(2,1)} %param.13), kind=kOutput, calls=%fused_computation.148 | convolution fusion | flops 4295491584 | bytes 13631488 | tf_op jit(solution)/shard_map/dot_general | solution.py:53
  536.1 9.7 %shard_map.123 = (bf16[512,1024]{1,0:T(8,128)(2,1)S(1)}, bf16[512,128]{1,0:T(8,128)(2,1)S(1)}, bf16[512,128]{1,0:T(8,128)(2,1)S(1)}) custom-call(bf16[512,1024]{1,0:T(8,128)(2,1)S(1)} %pad_maximum_fusion.8.gm_ref, bf16[512,1024]{1,0:T(8,128)(2,1)S(1)} %copy-done.23, bf16[512,128]{1,0:T(8,128)(2,1)S(1)} %copy-done.26, bf16[512,128]{1,0:T(8,128)(2,1)S(1)} %copy-done.29, ...), custom_call_target="tpu_custom_call" | custom-call | flops 2684354560 | bytes 7340032 | tf_op jit(solution)/shard_map/pallas_call | solution.py:157
  545.8 4.2 fusion
  550.1 4.2 fusion.6
  576.9 11.5 %collective-permute-start.38 = (bf16[128,4096]{1,0:T(8,128)(2,1)S(1)}, bf16[128,4096]{1,0:T(8,128)(2,1)S(1)}, u32[]{:S(2)}, u32[]{:S(2)}) collective-permute-start(bf16[128,4096]{1,0:T(8,128)(2,1)S(1)} %fusion.58), channel_id=1, source_target_pairs={{0,2},{1,3},{2,0},{3,1},{4,6},{5,7},{6,4},{7,5}} | collective-permute-start | bytes 3145736 | tf_op jit(solution)/shard_map/ppermute | solution.py:219
  591.4 51.0 %collective-permute-done.35 = bf16[512,128]{1,0:T(8,128)(2,1)S(1)} collective-permute-done((bf16[512,128]{1,0:T(8,128)(2,1)S(1)}, bf16[512,128]{1,0:T(8,128)(2,1)S(1)}, u32[]{:S(2)}, u32[]{:S(2)}) %collective-permute-start.35) | collective-permute-done | bytes 131104 | tf_op jit(solution)/shard_map/ppermute | solution.py:239
  646.6 7.3 %convolution_multiply_fusion = f32[2048,1024]{1,0:T(8,128)} fusion(bf16[1024,2048]{1,0:T(8,128)(2,1)S(1)} %pad_maximum_fusion.2, bf16[512,1024]{1,0:T(8,128)(2,1)S(1)} %collective-permute-done.34, bf16[512,1024]{1,0:T(8,128)(2,1)S(1)} %select_select_fusion.1), kind=kOutput, calls=%fused_computation.93 | convolution fusion | flops 4301258752 | bytes 14680064 | tf_op jit(solution)/shard_map/dot_general | solution.py:59
  653.9 6.9 %convolution_multiply_fusion.1 = f32[1024,2048]{1,0:T(8,128)} fusion(bf16[1024,1024]{1,0:T(8,128)(2,1)S(1)} %copy-done.57, bf16[512,2048]{1,0:T(8,128)(2,1)S(1)} %collective-permute-done.33, bf16[512,2048]{1,0:T(8,128)(2,1)S(1)} %get-tuple-element.63), kind=kOutput, calls=%fused_computation.94 | convolution fusion | flops 4305453056 | bytes 14680064 | tf_op jit(solution)/shard_map/dot_general | solution.py:59
  662.3 4.0 fusion.111
  (322 shorter events, 175.0 us)
Async XLA Ops:
  0.7 12.7 %collective-permute-start = (bf16[128,4096]{1,0:T(8,128)(2,1)}, bf16[128,4096]{1,0:T(8,128)(2,1)}, u32[]{:S(2)}, u32[]{:S(2)}) collective-permute-start(bf16[128,4096]{1,0:T(8,128)(2,1)} %param.14), channel_id=1, source_target_pairs={{24,25},{25,26},{26,27},{27,24},{28,29},{29,30},{30,31},{31,28}} | collective-permute-start | bytes 3145736 | tf_op jit(solution)/shard_map/ppermute | solution.py:219
  2.4 16.0 %collective-permute-start.1 = (bf16[128,4096]{1,0:T(8,128)(2,1)}, bf16[128,4096]{1,0:T(8,128)(2,1)}, u32[]{:S(2)}, u32[]{:S(2)}) collective-permute-start(bf16[128,4096]{1,0:T(8,128)(2,1)} %param.14), channel_id=1, source_target_pairs={{24,26},{25,27},{26,24},{27,25},{28,30},{29,31},{30,28},{31,29}} | collective-permute-start | bytes 3145736 | tf_op jit(solution)/shard_map/ppermute | solution.py:219
  4.1 14.4 %collective-permute-start.2 = (bf16[128,4096]{1,0:T(8,128)(2,1)}, bf16[128,4096]{1,0:T(8,128)(2,1)}, u32[]{:S(2)}, u32[]{:S(2)}) collective-permute-start(bf16[128,4096]{1,0:T(8,128)(2,1)} %param.14), channel_id=1, source_target_pairs={{24,27},{25,24},{26,25},{27,26},{28,31},{29,28},{30,29},{31,30}} | collective-permute-start | bytes 3145736 | tf_op jit(solution)/shard_map/ppermute | solution.py:219
  19.2 43.2 %collective-permute-start.6 = (f32[8,128]{1,0:T(8,128)S(1)}, f32[8,128]{1,0:T(8,128)S(1)}, u32[]{:S(2)}, u32[]{:S(2)}) collective-permute-start(f32[8,128]{1,0:T(8,128)S(1)} %convert_add_fusion), channel_id=1, source_target_pairs={{8,0},{9,1},{10,2},{11,3},{24,16},{25,17},{26,18},{27,19},{12,4},{... | collective-permute-start | bytes 12296 | tf_op jit(solution)/shard_map/ppermute | solution.py:268
  64.0 16.9 %collective-permute-start.7 = (bf16[128,4096]{1,0:T(8,128)(2,1)S(1)}, bf16[128,4096]{1,0:T(8,128)(2,1)S(1)}, u32[]{:S(2)}, u32[]{:S(2)}) collective-permute-start(bf16[128,4096]{1,0:T(8,128)(2,1)S(1)} %broadcast_add_fusion), channel_id=1, source_target_pairs={{0,1},{1,2},{2,3},{3,0},{16,17},{17,18},{18,19},{19,16},{4,5},{5,6... | collective-permute-start | bytes 3145736 | tf_op jit(solution)/shard_map/ppermute | solution.py:225
  73.1 38.8 %collective-permute-start.8 = (bf16[128,4096]{1,0:T(8,128)(2,1)S(1)}, bf16[128,4096]{1,0:T(8,128)(2,1)S(1)}, u32[]{:S(2)}, u32[]{:S(2)}) collective-permute-start(bf16[128,4096]{1,0:T(8,128)(2,1)S(1)} %broadcast_add_fusion), channel_id=1, source_target_pairs={{0,2},{1,3},{2,0},{3,1},{16,18},{17,19},{18,16},{19,17},{4,6},{5,7... | collective-permute-start | bytes 3145736 | tf_op jit(solution)/shard_map/ppermute | solution.py:225
  76.7 37.3 %collective-permute-start.9 = (bf16[128,4096]{1,0:T(8,128)(2,1)S(1)}, bf16[128,4096]{1,0:T(8,128)(2,1)S(1)}, u32[]{:S(2)}, u32[]{:S(2)}) collective-permute-start(bf16[128,4096]{1,0:T(8,128)(2,1)S(1)} %broadcast_add_fusion), channel_id=1, source_target_pairs={{0,3},{1,0},{2,1},{3,2},{16,19},{17,16},{18,17},{19,18},{4,7},{5,4... | collective-permute-start | bytes 3145736 | tf_op jit(solution)/shard_map/ppermute | solution.py:225
  146.7 13.7 %collective-permute-start.10 = (bf16[128,4096]{1,0:T(8,128)(2,1)S(1)}, bf16[128,4096]{1,0:T(8,128)(2,1)S(1)}, u32[]{:S(2)}, u32[]{:S(2)}) collective-permute-start(bf16[128,4096]{1,0:T(8,128)(2,1)S(1)} %fusion.44), channel_id=1, source_target_pairs={{24,25},{25,26},{26,27},{27,24},{28,29},{29,30},{30,31},{31,28}} | collective-permute-start | bytes 3145736 | tf_op jit(solution)/shard_map/ppermute | solution.py:219
  199.5 16.8 %collective-permute-start.17 = (bf16[128,4096]{1,0:T(8,128)(2,1)}, bf16[128,4096]{1,0:T(8,128)(2,1)}, u32[]{:S(2)}, u32[]{:S(2)}) collective-permute-start(bf16[128,4096]{1,0:T(8,128)(2,1)} %fusion.49), channel_id=1, source_target_pairs={{16,17},{17,18},{18,19},{19,16},{20,21},{21,22},{22,23},{23,20}} | collective-permute-start | bytes 3145736 | tf_op jit(solution)/shard_map/ppermute | solution.py:219
  203.0 13.3 %collective-permute-start.18 = (bf16[128,4096]{1,0:T(8,128)(2,1)}, bf16[128,4096]{1,0:T(8,128)(2,1)}, u32[]{:S(2)}, u32[]{:S(2)}) collective-permute-start(bf16[128,4096]{1,0:T(8,128)(2,1)} %fusion.50), channel_id=1, source_target_pairs={{16,18},{17,19},{18,16},{19,17},{20,22},{21,23},{22,20},{23,21}} | collective-permute-start | bytes 3145736 | tf_op jit(solution)/shard_map/ppermute | solution.py:219
  227.0 50.0 %collective-permute-start.28 = (bf16[512,2048]{1,0:T(8,128)(2,1)}, bf16[512,2048]{1,0:T(8,128)(2,1)}, u32[]{:S(2)}, u32[]{:S(2)}) collective-permute-start(bf16[512,2048]{1,0:T(8,128)(2,1)} %get-tuple-element.66), channel_id=1, source_target_pairs={{0,4},{4,0},{1,5},{5,1},{2,6},{6,2},{3,7},{7,3},{8,12},{12,8},{9,1... | collective-permute-start | bytes 6291464 | tf_op jit(solution)/shard_map/ppermute | solution.py:239
  260.2 11.3 %collective-permute-start.24 = (bf16[128,4096]{1,0:T(8,128)(2,1)S(1)}, bf16[128,4096]{1,0:T(8,128)(2,1)S(1)}, u32[]{:S(2)}, u32[]{:S(2)}) collective-permute-start(bf16[128,4096]{1,0:T(8,128)(2,1)S(1)} %fusion.54), channel_id=1, source_target_pairs={{8,9},{9,10},{10,11},{11,8},{12,13},{13,14},{14,15},{15,12}} | collective-permute-start | bytes 3145736 | tf_op jit(solution)/shard_map/ppermute | solution.py:219
  267.6 15.1 %collective-permute-start.29 = (bf16[512,1024]{1,0:T(8,128)(2,1)}, bf16[512,1024]{1,0:T(8,128)(2,1)}, u32[]{:S(2)}, u32[]{:S(2)}) collective-permute-start(bf16[512,1024]{1,0:T(8,128)(2,1)} %pad_maximum_fusion.7), channel_id=1, source_target_pairs={{0,4},{4,0},{1,5},{5,1},{2,6},{6,2},{3,7},{7,3},{8,12},{12,8},{9,1... | collective-permute-start | bytes 3145736 | tf_op jit(solution)/shard_map/ppermute | solution.py:239
  274.4 210.2 %collective-permute-start.27 = (bf16[128,4096]{1,0:T(8,128)(2,1)}, bf16[128,4096]{1,0:T(8,128)(2,1)}, u32[]{:S(2)}, u32[]{:S(2)}) collective-permute-start(bf16[128,4096]{1,0:T(8,128)(2,1)} %fusion.88), channel_id=1, source_target_pairs={{8,0},{9,1},{10,2},{11,3},{12,4},{13,5},{14,6},{15,7}} | collective-permute-start | bytes 3145736 | tf_op jit(solution)/shard_map/ppermute | solution.py:219
  275.7 211.2 %collective-permute-start.30 = (bf16[128,4096]{1,0:T(8,128)(2,1)}, bf16[128,4096]{1,0:T(8,128)(2,1)}, u32[]{:S(2)}, u32[]{:S(2)}) collective-permute-start(bf16[128,4096]{1,0:T(8,128)(2,1)} %fusion.88), channel_id=1, source_target_pairs={{8,1},{9,2},{10,3},{11,0},{12,5},{13,6},{14,7},{15,4}} | collective-permute-start | bytes 3145736 | tf_op jit(solution)/shard_map/ppermute | solution.py:219
  279.7 222.2 %collective-permute-start.31 = (bf16[128,4096]{1,0:T(8,128)(2,1)}, bf16[128,4096]{1,0:T(8,128)(2,1)S(1)}, u32[]{:S(2)}, u32[]{:S(2)}) collective-permute-start(bf16[128,4096]{1,0:T(8,128)(2,1)} %fusion.88), channel_id=1, source_target_pairs={{8,2},{9,3},{10,0},{11,1},{12,6},{13,7},{14,4},{15,5}} | collective-permute-start | bytes 3145736 | tf_op jit(solution)/shard_map/ppermute | solution.py:219
  281.0 243.3 %collective-permute-start.32 = (bf16[128,4096]{1,0:T(8,128)(2,1)}, bf16[128,4096]{1,0:T(8,128)(2,1)S(1)}, u32[]{:S(2)}, u32[]{:S(2)}) collective-permute-start(bf16[128,4096]{1,0:T(8,128)(2,1)} %fusion.88), channel_id=1, source_target_pairs={{8,3},{9,0},{10,1},{11,2},{12,7},{13,4},{14,5},{15,6}} | collective-permute-start | bytes 3145736 | tf_op jit(solution)/shard_map/ppermute | solution.py:219
  565.6 22.9 %collective-permute-start.36 = (bf16[512,128]{1,0:T(8,128)(2,1)S(1)}, bf16[512,128]{1,0:T(8,128)(2,1)S(1)}, u32[]{:S(2)}, u32[]{:S(2)}) collective-permute-start(bf16[512,128]{1,0:T(8,128)(2,1)S(1)} %select_select_fusion.2), channel_id=1, source_target_pairs={{0,4},{4,0},{1,5},{5,1},{2,6},{6,2},{3,7},{7,3},{8,12},{12,8},{9,1... | collective-permute-start | bytes 393224 | tf_op jit(solution)/shard_map/ppermute | solution.py:239
  571.5 75.1 %collective-permute-start.34 = (bf16[512,1024]{1,0:T(8,128)(2,1)S(1)}, bf16[512,1024]{1,0:T(8,128)(2,1)S(1)}, u32[]{:S(2)}, u32[]{:S(2)}) collective-permute-start(bf16[512,1024]{1,0:T(8,128)(2,1)S(1)} %select_select_fusion.1), channel_id=1, source_target_pairs={{0,4},{4,0},{1,5},{5,1},{2,6},{6,2},{3,7},{7,3},{8,12},{12,8},{9,1... | collective-permute-start | bytes 3145736 | tf_op jit(solution)/shard_map/ppermute | solution.py:239
  572.4 81.4 %collective-permute-start.33 = (bf16[512,2048]{1,0:T(8,128)(2,1)S(1)}, bf16[512,2048]{1,0:T(8,128)(2,1)S(1)}, u32[]{:S(2)}, u32[]{:S(2)}) collective-permute-start(bf16[512,2048]{1,0:T(8,128)(2,1)S(1)} %get-tuple-element.64), channel_id=1, source_target_pairs={{0,4},{4,0},{1,5},{5,1},{2,6},{6,2},{3,7},{7,3},{8,12},{12,8},{9,1... | collective-permute-start | bytes 6291464 | tf_op jit(solution)/shard_map/ppermute | solution.py:239
  574.5 86.3 %collective-permute-start.37 = (bf16[128,4096]{1,0:T(8,128)(2,1)S(1)}, bf16[128,4096]{1,0:T(8,128)(2,1)S(1)}, u32[]{:S(2)}, u32[]{:S(2)}) collective-permute-start(bf16[128,4096]{1,0:T(8,128)(2,1)S(1)} %fusion.57), channel_id=1, source_target_pairs={{0,1},{1,2},{2,3},{3,0},{4,5},{5,6},{6,7},{7,4}} | collective-permute-start | bytes 3145736 | tf_op jit(solution)/shard_map/ppermute | solution.py:219
  576.9 83.9 %collective-permute-start.38 = (bf16[128,4096]{1,0:T(8,128)(2,1)S(1)}, bf16[128,4096]{1,0:T(8,128)(2,1)S(1)}, u32[]{:S(2)}, u32[]{:S(2)}) collective-permute-start(bf16[128,4096]{1,0:T(8,128)(2,1)S(1)} %fusion.58), channel_id=1, source_target_pairs={{0,2},{1,3},{2,0},{3,1},{4,6},{5,7},{6,4},{7,5}} | collective-permute-start | bytes 3145736 | tf_op jit(solution)/shard_map/ppermute | solution.py:219
  588.5 53.9 %collective-permute-start.35 = (bf16[512,128]{1,0:T(8,128)(2,1)S(1)}, bf16[512,128]{1,0:T(8,128)(2,1)S(1)}, u32[]{:S(2)}, u32[]{:S(2)}) collective-permute-start(bf16[512,128]{1,0:T(8,128)(2,1)S(1)} %select_select_fusion.3), channel_id=1, source_target_pairs={{0,4},{4,0},{1,5},{5,1},{2,6},{6,2},{3,7},{7,3},{8,12},{12,8},{9,1... | collective-permute-start | bytes 393224 | tf_op jit(solution)/shard_map/ppermute | solution.py:239
  642.4 18.4 %collective-permute-start.39 = (bf16[128,4096]{1,0:T(8,128)(2,1)S(1)}, bf16[128,4096]{1,0:T(8,128)(2,1)S(1)}, u32[]{:S(2)}, u32[]{:S(2)}) collective-permute-start(bf16[128,4096]{1,0:T(8,128)(2,1)S(1)} %fusion.59), channel_id=1, source_target_pairs={{0,3},{1,0},{2,1},{3,2},{4,7},{5,4},{6,5},{7,6}} | collective-permute-start | bytes 3145736 | tf_op jit(solution)/shard_map/ppermute | solution.py:219
  (80 other events, 1347.5 us)
